TPU v7x, 32 devices: a whole 2x2x4 slice. The times are simulated.
32 devices in a mesh: groups: 2 (over y), expert: 4 (over z), head: 2 (over x), pair: 2 (over core).
Axes of the slice: x: 2, y: 2, z: 4, core: 2. Of those that a mesh axis runs over, the one named last changes fastest.
Arguments:
- resid: bfloat16 [1024, 4096], P(('groups', 'expert'), ('head', 'pair')), parts along dimension 0, may hold values from -12 to 12
- query: bfloat16 [1024, 4096], P(('groups', 'expert'), ('head', 'pair')), parts along dimension 0, may hold values from -48 to 48
- keyval: bfloat16 [2, 1024, 512], P(None, ('groups', 'expert'), 'head'), parts along dimension 1, may hold values from -8 to 8
- wo: bfloat16 [4096, 4096], P(('head', 'pair'), 'expert'), may hold values from -0.375 to 0.375
- norm_gain: float32 [4096], replicated, may hold values from 0.1 to 1.9
- w_gate: bfloat16 [4, 4096, 1024], P('expert', None, ('head', 'pair')), may hold values from -0.09375 to 0.09375
- w_up: bfloat16 [4, 4096, 1024], P('expert', None, ('head', 'pair')), may hold values from -0.09375 to 0.09375
- w_down: bfloat16 [4, 1024, 4096], P('expert', None, ('head', 'pair')), may hold values from -0.1875 to 0.1875
- expert_ids: int32 [1024, 2], P(('groups', 'expert')), parts along dimension 0, may hold values from 0 to 3, as said below
- slot_ids: int32 [1024, 2], P(('groups', 'expert')), parts along dimension 0, may hold values from 0 to 127, as said below
- route_weights: float32 [1024, 2], P(('groups', 'expert')), parts along dimension 0, may hold values from 0.1 to 0.6
Outputs:
- attn_hidden: bfloat16 [1024, 4096], P(('groups', 'expert'), ('head', 'pair')), parts along dimension 0
- expert_mix: bfloat16 [1024, 4096], P(('groups', 'expert'), ('head', 'pair')), parts along dimension 0
There are 2 independent parts, one for each index of `groups`. A program takes and returns all parts, laid end to end along the dimension named above; an argument that names none is the same for every part. Nothing has to cross between parts.
Inputs may be any that keep to these rules, and one draw needn't show every extreme that they name: `expert_ids`: each token names 2 different experts. Within each aligned block of 128 tokens no expert is named more than 128 times, and one expert, the same in every block of a draw, is named exactly 128 times in every block. `slot_ids`: within each aligned block of 128 tokens the routes to one expert hold the slots 0 to their count - 1, each once.
All inputs are finite; a program needn't handle non-finite values.
Results may differ from a plain program's by a relative error of at most 0.02.
Values may be sent and summed in bfloat16 or wider, within the bound.
A program may use at most 64 MiB of HBM per device.

v0:
```python
import math

import jax
import jax.numpy as jnp
from jax import lax
from jax.sharding import PartitionSpec as P

D = 4096
QUERY_HEADS = 32
KEY_VALUE_HEADS = 4
HEAD_WIDTH = 128
TOPK = 2


norm_eps = 1e-06


def expert_block(w_gate, w_up, w_down, slot_block):
    gate_val = jnp.einsum("ensd,edf->ensf", slot_block, w_gate, preferred_element_type=jnp.float32)
    up_val = jnp.einsum("ensd,edf->ensf", slot_block, w_up, preferred_element_type=jnp.float32)
    activated = (jax.nn.silu(gate_val) * up_val).astype(jnp.bfloat16)
    all_hidden = lax.all_gather(activated, ("head", "pair"), axis=3, tiled=True)
    return jnp.einsum(
        "ensf,efd->ensd", all_hidden, w_down, preferred_element_type=jnp.float32
    ).astype(jnp.bfloat16)


def body(
    resid, query, keyval, wo, norm_gain, w_gate, w_up, w_down, expert_ids, slot_ids, route_weights
):
    tok_rows = resid.shape[0]
    feature_cols = resid.shape[1]
    q_local = query.shape[1] // HEAD_WIDTH
    kv_local = keyval.shape[2] // HEAD_WIDTH
    heads_per_group = QUERY_HEADS // KEY_VALUE_HEADS
    query_pos = lax.axis_index("expert") * tok_rows + jnp.arange(tok_rows, dtype=jnp.int32)
    key_head = (
        lax.axis_index("pair") * q_local + jnp.arange(q_local, dtype=jnp.int32)
    ) // heads_per_group
    queries = query.reshape(tok_rows, q_local, HEAD_WIDTH)
    inverse_root = 1.0 / math.sqrt(HEAD_WIDTH)
    shards = lax.all_gather(keyval, "expert", axis=1, tiled=True)
    run_max = jnp.full((tok_rows, q_local), -1e30, jnp.float32)
    count = shards.shape[1]
    keys_here = jnp.take(shards[0].reshape(count, kv_local, HEAD_WIDTH), key_head, axis=1)
    values_here = jnp.take(shards[1].reshape(count, kv_local, HEAD_WIDTH), key_head, axis=1)
    scores = (
        jnp.einsum("thd,uhd->thu", queries, keys_here, preferred_element_type=jnp.float32)
        * inverse_root
    )
    key_pos = jnp.arange(count, dtype=jnp.int32)
    visible = (key_pos[None, :] <= query_pos[:, None])[:, None, :]
    scores = jnp.where(visible, scores, -jnp.inf)
    new_max = jnp.maximum(run_max, jnp.max(scores, axis=2))
    weights = jnp.where(visible, jnp.exp(scores - new_max[:, :, None]), 0.0)
    run_total = jnp.sum(weights, axis=2)
    weighted = jnp.einsum(
        "thu,uhd->thd",
        weights.astype(jnp.bfloat16),
        values_here,
        preferred_element_type=jnp.float32,
    )
    run_max, run_total, weighted = (new_max, run_total, weighted)
    heads_out = (
        (weighted / run_total[:, :, None])
        .astype(jnp.bfloat16)
        .reshape(tok_rows, q_local * HEAD_WIDTH)
    )
    partial_proj = jnp.dot(
        heads_out,
        lax.all_gather(wo, "expert", axis=1, tiled=True),
        preferred_element_type=jnp.float32,
    )
    attn_sum = lax.psum_scatter(
        partial_proj.astype(jnp.bfloat16), ("head", "pair"), scatter_dimension=1, tiled=True
    ).astype(jnp.float32)
    attn_hidden = (resid.astype(jnp.float32) + attn_sum).astype(jnp.bfloat16)
    experts_here = w_gate.shape[0]
    experts_all = experts_here * lax.axis_size("expert")
    capacity = 2 * tok_rows * TOPK // experts_all
    target = expert_ids * capacity + slot_ids
    slot_index = jnp.arange(experts_all * capacity, dtype=jnp.int32)
    placing = jnp.sum(
        (target[None, :, :] == slot_index[:, None, None]).astype(jnp.int32), axis=2
    ).astype(jnp.bfloat16)
    row_floats = attn_hidden.astype(jnp.float32)
    square_sum = lax.psum(jnp.sum(row_floats * row_floats, axis=1), ("head", "pair"))
    mean_square = (square_sum / D)[:, None]
    shard_index = lax.axis_index("head") * lax.axis_size("pair") + lax.axis_index("pair")
    gain_part = lax.dynamic_slice_in_dim(norm_gain, shard_index * feature_cols, feature_cols)
    normed = (row_floats * lax.rsqrt(mean_square + norm_eps) * gain_part).astype(jnp.bfloat16)
    filled = jnp.dot(placing, normed, preferred_element_type=jnp.float32).astype(jnp.bfloat16)
    whole_rows = lax.all_gather(
        lax.all_to_all(
            filled.reshape(experts_all, 1, capacity, normed.shape[1]),
            "expert",
            split_axis=0,
            concat_axis=1,
            tiled=True,
        ),
        ("head", "pair"),
        axis=3,
        tiled=True,
    )
    expert_out = expert_block(w_gate, w_up, w_down, whole_rows)
    returned = lax.all_to_all(expert_out, "expert", split_axis=1, concat_axis=0, tiled=True)
    returned = returned.reshape(experts_all * capacity, feature_cols)
    picked = jnp.take(returned, target.reshape(-1), axis=0).reshape(tok_rows, TOPK, feature_cols)
    expert_mix = jnp.sum(route_weights[:, :, None] * picked.astype(jnp.float32), axis=1).astype(
        jnp.bfloat16
    )
    return (attn_hidden, expert_mix)


def solution(mesh):
    return jax.shard_map(
        body,
        mesh=mesh,
        in_specs=(
            P(("groups", "expert"), ("head", "pair")),
            P(("groups", "expert"), ("head", "pair")),
            P(None, ("groups", "expert"), "head"),
            P(("head", "pair"), "expert"),
            P(),
            P("expert", None, ("head", "pair")),
            P("expert", None, ("head", "pair")),
            P("expert", None, ("head", "pair")),
            P(("groups", "expert"), None),
            P(("groups", "expert"), None),
            P(("groups", "expert"), None),
        ),
        out_specs=(
            P(("groups", "expert"), ("head", "pair")),
            P(("groups", "expert"), ("head", "pair")),
        ),
        check_vma=False,
    )
```

profile of v0, /device:TPU:25, one launch (start us, length us, event | category | flops | bytes accessed | tf_op | source)
XLA Modules:
  0.0 327.7 jit_solution(5293731449320666742)
XLA Ops:
  7.2 0.0 copy-start
  7.2 0.0 copy-start.4
  7.2 0.0 all-gather.6.cloned.1.call-start
  7.2 0.7 all-gather.6.cloned.1.call-update
  7.9 0.0 reduce-scatter.2.cloned.1.call-start
  8.0 0.3 copy-done.4
  8.2 0.1 copy.48
  8.4 11.0 %all_gather.12 = bf16[2,512,256]{1,2,0:T(8,128)(2,1)S(1)} all-gather(bf16[2,128,256]{1,2,0:T(8,128)(2,1)S(1)} %copy.48), channel_id=1, replica_groups=mesh['groups'=2,'expert'=4,'head'=2,'pair'=2] {'expert'}, dimensions={1}, use_global_device_ids=true | all-gather | bytes 655360 | tf_op jit(solution)/shard_map/all_gather | solution.py:42
  19.4 0.2 copy.50
  19.6 0.2 copy.49
  19.8 0.0 copy-start.10
  19.8 1.7 gather_fusion.2
  21.6 1.6 gather_fusion.1
  23.3 0.0 copy-done.10
  23.3 1.9 fusion.8
  25.1 0.0 copy-start.1
  25.2 0.5 fusion.12
  25.7 0.7 copy-done.1
  26.4 1.0 fusion.28
  27.4 130.6 %all-gather.6.cloned.1.call-done = bf16[1024,4096]{1,0:T(8,128)(2,1)} async-done(((bf16[1024,1024]{1,0:T(8,128)(2,1)}), bf16[1024,4096]{1,0:T(8,128)(2,1)}) %all-gather.6.cloned.1.call-update) | async-done | bytes 8388624 | tf_op jit(solution)/shard_map/all_gather | solution.py:71
  157.9 0.0 copy-start.6
  157.9 0.0 copy-start.7
  157.9 0.0 copy-start.3
  158.0 5.8 %convolution_convert_fusion = bf16[128,4096]{1,0:T(8,128)(2,1)} fusion(bf16[128,1024]{0,1:T(8,128)(2,1)S(1)} %bitcast.84, bf16[1024,4096]{1,0:T(8,128)(2,1)} %all-gather.6.cloned.1.call-done), kind=kOutput, calls=%fused_computation.3 | convolution fusion | flops 1074266112 | bytes 9699328 | tf_op jit(solution)/shard_map/dot_general | solution.py:69
  163.7 0.0 reduce-scatter.2.cloned.1.call-update
  163.7 0.0 all-gather.8.cloned.1.call-start
  163.8 0.7 dynamic_slice.3
  164.5 0.0 copy-done.6
  164.5 0.0 copy-done.7
  164.5 0.1 convert_reduce_fusion
  164.6 25.1 %reduce-scatter.2.cloned.1.call-done = bf16[128,1024]{1,0:T(8,128)(2,1)} async-done(((bf16[128,4096]{1,0:T(8,128)(2,1)}), bf16[128,1024]{1,0:T(8,128)(2,1)}) %reduce-scatter.2.cloned.1.call-update) | async-done | bytes 262160 | tf_op jit(solution)/shard_map/reduce_scatter | solution.py:74
  189.7 0.0 copy-done.3
  189.7 1.1 fusion.42
  190.8 0.0 copy-start.2
  190.8 5.7 %psum.7 = f32[128]{0:T(128)S(1)} all-reduce(f32[128]{0:T(128)S(1)} %get-tuple-element.5), channel_id=1, replica_groups=mesh['groups'=2,'expert'=4,'head'=2,'pair'=2] {'head','pair'}, use_global_device_ids=true, to_apply=%region_5.7 | all-reduce | flops 128 | bytes 1024 | tf_op jit(solution)/shard_map/psum | solution.py:87
  196.6 0.5 convolution_convert_fusion.1
  197.1 27.9 %all_to_all.21 = bf16[4,1,128,1024]{3,2,1,0:T(8,128)(2,1)} all-to-all(bf16[4,1,128,1024]{3,2,1,0:T(8,128)(2,1)S(1)} %bitcast.81), channel_id=1, replica_groups=mesh['groups'=2,'expert'=4,'head'=2,'pair'=2] {'expert'}, dimensions={0} | all-to-all | bytes 2097152 | tf_op jit(solution)/shard_map/all_to_all | solution.py:94
  225.0 0.0 all-gather.8.cloned.1.call-update
  225.0 0.0 copy-done.2
  225.0 0.0 all-gather.10.cloned.1.call-start
  225.1 35.5 %all-gather.8.cloned.1.call-done = bf16[4,1,128,4096]{3,2,0,1:T(8,128)(2,1)} async-done(((bf16[4,1,128,1024]{3,2,0,1:T(8,128)(2,1)}), bf16[4,1,128,4096]{3,2,0,1:T(8,128)(2,1)}) %all-gather.8.cloned.1.call-update) | async-done | bytes 4194320 | tf_op jit(solution)/shard_map/all_gather | solution.py:93
  260.5 0.0 copy-start.8
  260.5 0.0 copy-start.9
  260.5 4.2 %fusion.2 = f32[4,128,256]{2,1,0:T(8,128)S(1)} fusion(bf16[4,1,128,4096]{3,2,0,1:T(8,128)(2,1)} %all-gather.8.cloned.1.call-done, bf16[1,4096,256]{2,1,0:T(8,128)(2,1)} %param.18), kind=kOutput, calls=%fused_computation.6 | convolution fusion | flops 1073741824 | bytes 6815744 | tf_op jit(solution)/shard_map/ensd,edf->ensf/dot_general | solution.py:19
  264.8 0.0 copy-done.8
  264.8 0.5 copy-done.9
  265.3 2.0 fusion.23
  267.2 0.0 all-gather.10.cloned.1.call-update
  267.2 17.0 %all-gather.10.cloned.1.call-done = bf16[4,128,1024]{2,1,0:T(8,128)(2,1)} async-done(((bf16[4,128,256]{2,1,0:T(8,128)(2,1)}), bf16[4,128,1024]{2,1,0:T(8,128)(2,1)}) %all-gather.10.cloned.1.call-update) | async-done | bytes 1048592 | tf_op jit(solution)/shard_map/all_gather | solution.py:22
  284.2 0.0 copy-done
  284.2 3.5 %fusion.14 = bf16[1,4,128,1024]{3,2,0,1:T(8,128)(2,1)} fusion(bf16[4,128,1024]{2,1,0:T(8,128)(2,1)} %all-gather.10.cloned.1.call-done, bf16[1,1024,1024]{2,1,0:T(8,128)(2,1)S(1)} %copy-done), kind=kOutput, calls=%fused_computation.19 | convolution fusion | flops 1074266112 | bytes 4194304 | tf_op jit(solution)/shard_map/ensf,efd->ensd/dot_general | solution.py:23
  287.7 0.0 copy-start.5
  287.7 4.7 %all-to-all-start.1 = ((bf16[1,4,128,1024]{3,2,0,1:T(8,128)(2,1)}), bf16[1,4,128,1024]{3,2,0,1:T(8,128)(2,1)S(1)}, u32[]{:S(2)}, u32[]{:S(2)}) async-start(bf16[1,4,128,1024]{3,2,0,1:T(8,128)(2,1)} %fusion.14), calls=%async_computation.2 | async-start | bytes 2097152 | tf_op jit(solution)/shard_map/all_to_all | solution.py:106
  292.4 0.1 copy.59
  292.5 0.1 reshape.138
  292.7 0.1 copy.55
  292.8 0.0 copy-done.5
  292.8 0.1 copy.54
  292.9 22.7 %all-to-all-done.1 = bf16[1,4,128,1024]{3,2,0,1:T(8,128)(2,1)S(1)} async-done(((bf16[1,4,128,1024]{3,2,0,1:T(8,128)(2,1)}), bf16[1,4,128,1024]{3,2,0,1:T(8,128)(2,1)S(1)}, u32[]{:S(2)}, u32[]{:S(2)}) %all-to-all-start.1) | async-done | bytes 1048608 | tf_op jit(solution)/shard_map/all_to_all | solution.py:106
  315.6 2.0 gather_fusion
  317.6 1.2 gather.10
  318.8 2.4 multiply_reduce_fusion
  (11 shorter events, 0.2 us)
Async XLA Ops:
  7.2 277.1 %copy-start = (bf16[1,1024,1024]{2,1,0:T(8,128)(2,1)S(1)}, bf16[1,1024,1024]{2,1,0:T(8,128)(2,1)}, u32[]{:S(2)}) copy-start(bf16[1,1024,1024]{2,1,0:T(8,128)(2,1)} %param.20) | copy-start | bytes 6291460
  7.2 1.1 copy-start.4
  7.2 150.8 %all-gather.6.cloned.1.call-start = ((), (), s32[]{:S(2)}) async-start(), calls=%async_computation.3 | async-start | bytes 10485760 | tf_op jit(solution)/shard_map/all_gather | solution.py:71
  7.9 181.8 %reduce-scatter.2.cloned.1.call-start = ((), (), s32[]{:S(2)}) async-start(), calls=%async_computation.4 | async-start | bytes 1310720 | tf_op jit(solution)/shard_map/reduce_scatter | solution.py:74
  19.8 3.5 %copy-start.10 = (bf16[128,1024]{1,0:T(8,128)(2,1)S(1)}, bf16[128,1024]{1,0:T(8,128)(2,1)}, u32[]{:S(2)}) copy-start(bf16[128,1024]{1,0:T(8,128)(2,1)} %param.14) | copy-start | bytes 786436
  25.1 1.2 copy-start.1
  157.9 6.6 %copy-start.6 = (s32[128,2]{0,1:T(2,128)S(1)}, s32[128,2]{0,1:T(2,128)}, u32[]{:S(2)}) copy-start(s32[128,2]{0,1:T(2,128)} %param.22) | copy-start | bytes 3076
  157.9 6.6 %copy-start.7 = (s32[128,2]{0,1:T(2,128)S(1)}, s32[128,2]{0,1:T(2,128)}, u32[]{:S(2)}) copy-start(s32[128,2]{0,1:T(2,128)} %param.21) | copy-start | bytes 3076
  157.9 31.7 %copy-start.3 = (bf16[128,1024]{1,0:T(8,128)(2,1)S(1)}, bf16[128,1024]{1,0:T(8,128)(2,1)}, u32[]{:S(2)}) copy-start(bf16[128,1024]{1,0:T(8,128)(2,1)} %param.13) | copy-start | bytes 786436
  163.7 96.8 %all-gather.8.cloned.1.call-start = ((), (), s32[]{:S(2)}) async-start(), calls=%async_computation.5 | async-start | bytes 5242880 | tf_op jit(solution)/shard_map/all_gather | solution.py:93
  190.8 34.2 %copy-start.2 = (bf16[128,1024]{1,0:T(8,128)(2,1)}, bf16[128,1024]{1,0:T(8,128)(2,1)S(1)}, u32[]{:S(2)}) copy-start(bf16[128,1024]{1,0:T(8,128)(2,1)S(1)} %get-tuple-element.6) | copy-start | bytes 786436
  225.0 59.2 %all-gather.10.cloned.1.call-start = ((), (), s32[]{:S(2)}) async-start(), calls=%async_computation.6 | async-start | bytes 1310720 | tf_op jit(solution)/shard_map/all_gather | solution.py:22
  260.5 4.3 %copy-start.8 = (bf16[4,1,128,4096]{3,2,0,1:T(8,128)(2,1)S(1)}, bf16[4,1,128,4096]{3,2,0,1:T(8,128)(2,1)}, u32[]{:S(2)}) copy-start(bf16[4,1,128,4096]{3,2,0,1:T(8,128)(2,1)} %all-gather.8.cloned.1.call-done) | copy-start | bytes 12582916
  260.5 4.7 %copy-start.9 = (bf16[1,4096,256]{2,1,0:T(8,128)(2,1)S(1)}, bf16[1,4096,256]{2,1,0:T(8,128)(2,1)}, u32[]{:S(2)}) copy-start(bf16[1,4096,256]{2,1,0:T(8,128)(2,1)} %param.19) | copy-start | bytes 6291460
  287.7 5.1 %copy-start.5 = (f32[128,2]{0,1:T(2,128)S(1)}, f32[128,2]{0,1:T(2,128)}, u32[]{:S(2)}) copy-start(f32[128,2]{0,1:T(2,128)} %param.23) | copy-start | bytes 3076
  287.7 27.9 %all-to-all-start.1 = ((bf16[1,4,128,1024]{3,2,0,1:T(8,128)(2,1)}), bf16[1,4,128,1024]{3,2,0,1:T(8,128)(2,1)S(1)}, u32[]{:S(2)}, u32[]{:S(2)}) async-start(bf16[1,4,128,1024]{3,2,0,1:T(8,128)(2,1)} %fusion.14), calls=%async_computation.2 | async-start | bytes 2097152 | tf_op jit(solution)/shard_map/all_to_all | solution.py:106
Sparse Core Ops, SparseCore 0:
  9.6 148.3 all-gather.5
  163.9 25.7 reduce-scatter.1
  225.1 35.3 all-gather.7
  267.4 16.8 all-gather.9
where the time goes:
time: 333 us; the launch traced here: 328 us
  waiting for transfers between devices  232 us (70%)
  blocking collectives  44.6 us (13%)
  matrix products  18.8 us (6%)
  between operations  14 us (4%)
  local copies, waits for them, and re-layouts  9.72 us (3%)
  starting transfers between devices  4.82 us (1%)
  other arithmetic  4.17 us (1%)
    all_gather x1, waiting for transfers between devices, body(): lax.all_gather(wo, 'expert', axis=1, tiled=True)  131 us
    all_gather x1, waiting for transfers between devices, body(): lax.all_gather(lax.all_to_all(filled.reshape(experts_all, 1, capacity, no...  35.5 us
    all_to_all x1, blocking collectives, body(): lax.all_to_all(filled.reshape(experts_all, 1, capacity, normed.shape[1]),...  27.9 us
    reduce_scatter x1, waiting for transfers between devices, body(): lax.psum_scatter(partial_proj.astype(jnp.bfloat16), ('head', 'pair'), sca...  25.1 us
    all_to_all x1, waiting for transfers between devices, body(): lax.all_to_all(expert_out, 'expert', split_axis=1, concat_axis=0, tiled=T...  22.7 us
    all_gather x1, waiting for transfers between devices, expert_block(): all_hidden = lax.all_gather(activated, ('head', 'pair'), axis=3, tiled=True)  17 us
    all_gather x1, blocking collectives, body(): shards = lax.all_gather(keyval, 'expert', axis=1, tiled=True)  11 us
  transfers between devices with their start and end apart: 5, of which 5 were waited for; matrix products, arithmetic and copies ran while one was open for 3% of the time, Pallas kernels for 0%

commit v1 on v0

--- a/solution.py
+++ b/solution.py
@@ -1,8 +1,11 @@
+import functools
 import math
 
 import jax
 import jax.numpy as jnp
 from jax import lax
+from jax.experimental import pallas as pl
+from jax.experimental.pallas import tpu as pltpu
 from jax.sharding import PartitionSpec as P
 
 D = 4096
@@ -25,7 +28,7 @@
     ).astype(jnp.bfloat16)
 
 
-def body(
+def slotted_body(
     resid, query, keyval, wo, norm_gain, w_gate, w_up, w_down, expert_ids, slot_ids, route_weights
 ):
     tok_rows = resid.shape[0]
@@ -112,6 +115,335 @@
     return (attn_hidden, expert_mix)
 
 
+MESH = pl.DeviceIdType.MESH
+
+
+def fused_kernel(
+    nz, nx, npair, q_ref, kv_ref, resid_ref, gain_ref, ids_ref, rw_ref, wo_hbm, wg_hbm, wu_hbm, wd_hbm,
+    hid_ref, mix_ref,
+    wo, wgu, wd, kv_all, ho, pbuf, pin, resid_t, xall, act_all, eo, ret,
+    w_sem, self_sem, kv_s, kv_r, rs_s, rs_r, ho_s, ho_r, p_s, p_r, z_s, z_r, x_s, x_r, c_s, c_r, f_s, f_r,
+    a_s, a_r, e_s, e_r,
+):
+    nhp = nx * npair
+    g, z = lax.axis_index("groups"), lax.axis_index("expert")
+    x, p = lax.axis_index("head"), lax.axis_index("pair")
+    hp = x * npair + p
+    rows, cols = q_ref.shape
+    part_rows = rows // nhp
+    hidden = wg_hbm.shape[2]
+    heads = cols // HEAD_WIDTH
+    f32, bf16 = jnp.float32, jnp.bfloat16
+
+    def at(zt, hpt):
+        return (g, zt, hpt // npair, lax.rem(hpt, npair))
+
+    def remote(src, dst, ssem, rsem, dev):
+        return pltpu.make_async_remote_copy(
+            src_ref=src, dst_ref=dst, send_sem=ssem, recv_sem=rsem, device_id=dev, device_id_type=MESH
+        )
+
+    def slab(index):
+        return pl.ds(pl.multiple_of(index * part_rows, part_rows), part_rows)
+
+    mine = slab(hp)
+    z_others = [lax.rem(z + d, nz) for d in range(1, nz)]
+    hp_others = [lax.rem(hp + d, nhp) for d in range(1, nhp)]
+    x_dev = (g, z, 1 - x, p)
+    c_dev = (g, z, x, 1 - p)
+    hp_x = (1 - x) * npair + p
+    hp_c = x * npair + 1 - p
+    hp_xc = (1 - x) * npair + 1 - p
+
+    weights = [
+        pltpu.make_async_copy(wo_hbm, wo, w_sem.at[0]),
+        pltpu.make_async_copy(wg_hbm.at[0], wgu.at[:, 0:hidden], w_sem.at[1]),
+        pltpu.make_async_copy(wu_hbm.at[0], wgu.at[:, hidden : 2 * hidden], w_sem.at[2]),
+        pltpu.make_async_copy(wd_hbm.at[0], wd, w_sem.at[3]),
+    ]
+    for copy in weights:
+        copy.start()
+    kv_all[z] = kv_ref[:, :, pl.ds(pl.multiple_of(p * HEAD_WIDTH, HEAD_WIDTH), HEAD_WIDTH)]
+
+    barrier = pltpu.get_barrier_semaphore()
+    for dz in range(nz):
+        for dh in range(nhp):
+            if dz or dh:
+                pl.semaphore_signal(
+                    barrier,
+                    inc=1,
+                    device_id=at(lax.rem(z + dz, nz), lax.rem(hp + dh, nhp)),
+                    device_id_type=MESH,
+                )
+    pl.semaphore_wait(barrier, nz * nhp - 1)
+
+    def kv_copy(i, zt):
+        return remote(kv_all.at[z], kv_all.at[z], kv_s.at[i], kv_r.at[z], at(zt, hp))
+
+    for d in range(nz - 1, 0, -1):
+        @pl.when(z + d < nz)
+        def _():
+            kv_copy(d, lax.rem(z + d, nz)).start()
+
+    def resid_copy(j):
+        return remote(resid_ref.at[pl.ds(j * part_rows, part_rows)], resid_t.at[z], rs_s.at[j], rs_r.at[z], at(hp, j))
+
+    for j in range(nhp):
+        is_self = jnp.logical_and(z == hp, hp == j)
+
+        @pl.when(jnp.logical_not(is_self))
+        def _():
+            resid_copy(j).start()
+
+        @pl.when(is_self)
+        def _():
+            resid_t[z] = resid_ref[pl.ds(j * part_rows, part_rows), :]
+
+    scale = 1.0 / math.sqrt(HEAD_WIDTH)
+    for n in range(nz):
+        @pl.when(z == n)
+        def _():
+            for b in range(n):
+                remote(kv_all.at[b], kv_all.at[b], kv_s.at[0], kv_r.at[b], at(b, hp)).wait_recv()
+            count = (n + 1) * rows
+            keys = kv_all[0 : n + 1, 0].reshape(count, HEAD_WIDTH)
+            values = kv_all[0 : n + 1, 1].reshape(count, HEAD_WIDTH)
+            row = lax.broadcasted_iota(jnp.int32, (rows, count), 0) + n * rows
+            col = lax.broadcasted_iota(jnp.int32, (rows, count), 1)
+            visible = col <= row
+            for h in range(heads):
+                span = slice(h * HEAD_WIDTH, (h + 1) * HEAD_WIDTH)
+                scores = lax.dot_general(
+                    q_ref[:, span], keys, (((1,), (1,)), ((), ())), preferred_element_type=f32
+                )
+                scores = jnp.where(visible, scores * scale, -jnp.inf)
+                probs = jnp.exp(scores - jnp.max(scores, axis=1, keepdims=True))
+                total = jnp.sum(probs, axis=1, keepdims=True)
+                mixed = jnp.dot(probs.astype(bf16), values, preferred_element_type=f32)
+                ho[n, :, span] = (mixed / total).astype(bf16)
+
+    def ho_copy(i):
+        return remote(ho.at[z], ho.at[z], ho_s.at[i], ho_r.at[z], at(z_others[i], hp))
+
+    for i in range(nz - 1):
+        ho_copy(i).start()
+    weights[0].wait()
+
+    def p_copy(b, i):
+        return remote(pbuf.at[b, slab(hp_others[i])], pin.at[b, hp], p_s.at[b, i], p_r.at[b, hp], at(z, hp_others[i]))
+
+    def z_copy(b, i):
+        return remote(
+            xall.at[b, z, mine], xall.at[b, z, mine], z_s.at[b, i], z_r.at[b, z], at(z_others[i], hp)
+        )
+
+    def group_copy(b, owner, ssem, rsem, dev):
+        ref = xall.at[b, :, slab(owner)]
+        return remote(ref, ref, ssem.at[b], rsem.at[b], dev)
+
+    def a_copy(b, i):
+        return remote(act_all.at[b, hp], act_all.at[b, hp], a_s.at[b, i], a_r.at[b, hp], at(z, hp_others[i]))
+
+    def e_copy(b):
+        return remote(eo.at[b], ret.at[z], e_s.at[b], e_r.at[z], at(b, hp))
+
+    def project(b):
+        @pl.when(z != b)
+        def _():
+            remote(ho.at[b], ho.at[b], ho_s.at[0], ho_r.at[b], at(b, hp)).wait_recv()
+
+        pbuf[b] = jnp.dot(ho[b], wo[...], preferred_element_type=f32).astype(bf16)
+        for i in range(nhp - 1):
+            p_copy(b, i).start()
+
+    def add_up(b):
+        @pl.when(jnp.logical_not(jnp.logical_and(z == b, hp == z)))
+        def _():
+            remote(
+                resid_ref.at[pl.ds(0, part_rows)], resid_t.at[b], rs_s.at[0], rs_r.at[b], at(b, z)
+            ).wait_recv()
+
+        for other in hp_others:
+            remote(pbuf.at[b, mine], pin.at[b, other], p_s.at[b, 0], p_r.at[b, other], at(z, other)).wait_recv()
+        total = pbuf[b, mine, :].astype(f32)
+        for other in hp_others:
+            total = total + pin[b, other].astype(f32)
+        xall[b, z, mine, :] = (resid_t[b].astype(f32) + total).astype(bf16)
+        for i in range(nz - 1):
+            z_copy(b, i).start()
+
+    def spread(b):
+        for other in z_others:
+            ref = xall.at[b, other, mine]
+            remote(ref, ref, z_s.at[b, 0], z_r.at[b, other], at(other, hp)).wait_recv()
+        group_copy(b, hp, x_s, x_r, x_dev).start()
+        group_copy(b, hp, c_s, c_r, c_dev).start()
+
+    def hidden_units(b):
+        group_copy(b, hp_x, x_s, x_r, x_dev).wait_recv()
+        group_copy(b, hp_x, f_s, f_r, c_dev).start()
+        group_copy(b, hp_c, c_s, c_r, c_dev).wait_recv()
+        group_copy(b, hp_xc, f_s, f_r, c_dev).wait_recv()
+        square = jnp.zeros((rows, 1), f32)
+        for e in range(nz):
+            part = xall[b, e].astype(f32)
+            square = square + jnp.sum(part * part, axis=1, keepdims=True)
+        root = lax.rsqrt(square / D + norm_eps)
+        both = jnp.zeros((rows, 2 * hidden), f32)
+        for e in range(nz):
+            normed = (xall[b, e].astype(f32) * root * gain_ref[e]).astype(bf16)
+            both = both + jnp.dot(normed, wgu[e * cols : (e + 1) * cols, :], preferred_element_type=f32)
+        gate, up = both[:, :hidden], both[:, hidden:]
+        act_all[b, hp] = (gate / (1.0 + jnp.exp(-gate)) * up).astype(bf16)
+        for i in range(nhp - 1):
+            a_copy(b, i).start()
+
+    def down(b):
+        for other in hp_others:
+            ref = act_all.at[b, other]
+            remote(ref, ref, a_s.at[b, 0], a_r.at[b, other], at(z, other)).wait_recv()
+        total = jnp.zeros((rows, cols), f32)
+        for j in range(nhp):
+            total = total + jnp.dot(
+                act_all[b, j], wd[j * hidden : (j + 1) * hidden, :], preferred_element_type=f32
+            )
+        eo[b] = total.astype(bf16)
+
+        @pl.when(z != b)
+        def _():
+            e_copy(b).start()
+
+    for step in range(nz + 4):
+        if step < nz:
+            project(step)
+        if 0 <= step - 1 < nz:
+            add_up(step - 1)
+        if 0 <= step - 2 < nz:
+            spread(step - 2)
+        if 0 <= step - 3 < nz:
+            if step == 3:
+                weights[1].wait()
+                weights[2].wait()
+            hidden_units(step - 3)
+        if 0 <= step - 4 < nz:
+            if step == 4:
+                weights[3].wait()
+            down(step - 4)
+
+    hid_ref[...] = xall[z, hp]
+    mix = route_share(ids_ref, rw_ref, z) * eo[z].astype(f32)
+    for other in z_others:
+        remote(eo.at[0], ret.at[other], e_s.at[0], e_r.at[other], at(other, hp)).wait_recv()
+        mix = mix + route_share(ids_ref, rw_ref, other) * ret[other].astype(f32)
+    mix_ref[...] = mix.astype(bf16)
+
+    for d in range(1, nz):
+        @pl.when(z + d < nz)
+        def _():
+            kv_copy(d, lax.rem(z + d, nz)).wait_send()
+
+    for j in range(nhp):
+        @pl.when(jnp.logical_not(jnp.logical_and(z == hp, hp == j)))
+        def _():
+            resid_copy(j).wait_send()
+
+    for i in range(nz - 1):
+        ho_copy(i).wait_send()
+    for b in range(nz):
+        for i in range(nhp - 1):
+            p_copy(b, i).wait_send()
+            a_copy(b, i).wait_send()
+        for i in range(nz - 1):
+            z_copy(b, i).wait_send()
+        group_copy(b, hp, x_s, x_r, x_dev).wait_send()
+        group_copy(b, hp, c_s, c_r, c_dev).wait_send()
+        group_copy(b, hp_x, f_s, f_r, c_dev).wait_send()
+
+        @pl.when(z != b)
+        def _():
+            e_copy(b).wait_send()
+
+
+def route_share(ids_ref, rw_ref, expert):
+    return jnp.sum(jnp.where(ids_ref[...] == expert, rw_ref[...], 0.0), axis=1, keepdims=True)
+
+
+def fused_body(
+    resid, query, keyval, wo, norm_gain, w_gate, w_up, w_down, expert_ids, slot_ids, route_weights
+):
+    nz, nx, npair = (lax.axis_size(name) for name in ("expert", "head", "pair"))
+    nhp = nx * npair
+    rows, cols = resid.shape
+    part_rows = rows // nhp
+    hidden = w_gate.shape[2]
+    bf16 = jnp.bfloat16
+    dma = pltpu.SemaphoreType.DMA
+    vmem = pl.BlockSpec(memory_space=pltpu.VMEM)
+    anywhere = pl.BlockSpec(memory_space=pl.ANY)
+    out = jax.ShapeDtypeStruct((rows, cols), bf16)
+    tokens = nz * rows
+    flops = 2 * tokens * (wo.shape[0] * cols + 2 * w_gate.shape[1] * hidden + w_down.shape[1] * cols)
+    return pl.pallas_call(
+        functools.partial(fused_kernel, nz, nx, npair),
+        out_shape=(out, out),
+        in_specs=[vmem] * 6 + [anywhere] * 4,
+        out_specs=(vmem, vmem),
+        scratch_shapes=[
+            pltpu.VMEM(wo.shape, bf16),
+            pltpu.VMEM((w_gate.shape[1], 2 * hidden), bf16),
+            pltpu.VMEM(w_down.shape[1:], bf16),
+            pltpu.VMEM((nz, 2, rows, HEAD_WIDTH), bf16),
+            pltpu.VMEM((nz, rows, cols), bf16),
+            pltpu.VMEM((nz, rows, cols), bf16),
+            pltpu.VMEM((nz, nhp, part_rows, cols), bf16),
+            pltpu.VMEM((nz, part_rows, cols), bf16),
+            pltpu.VMEM((nz, nz, rows, cols), bf16),
+            pltpu.VMEM((nz, nhp, rows, hidden), bf16),
+            pltpu.VMEM((nz, rows, cols), bf16),
+            pltpu.VMEM((nz, rows, cols), bf16),
+            dma((4,)),
+            dma((1,)),
+            dma((nz,)), dma((nz,)),
+            dma((nhp,)), dma((nz,)),
+            dma((nz,)), dma((nz,)),
+            dma((nz, nhp)), dma((nz, nhp)),
+            dma((nz, nz)), dma((nz, nz)),
+            dma((nz,)), dma((nz,)),
+            dma((nz,)), dma((nz,)),
+            dma((nz,)), dma((nz,)),
+            dma((nz, nhp)), dma((nz, nhp)),
+            dma((nz,)), dma((nz,)),
+        ],
+        compiler_params=pltpu.CompilerParams(
+            collective_id=0, has_side_effects=True, vmem_limit_bytes=48 * 1024 * 1024
+        ),
+        cost_estimate=pl.CostEstimate(
+            flops=flops, bytes_accessed=2 * (wo.size + 3 * w_gate.size), transcendentals=0
+        ),
+    )(
+        query, keyval, resid, norm_gain.reshape(nz, 1, cols), expert_ids, route_weights, wo, w_gate, w_up, w_down
+    )
+
+
+def body(
+    resid, query, keyval, wo, norm_gain, w_gate, w_up, w_down, expert_ids, slot_ids, route_weights
+):
+    args = (resid, query, keyval, wo, norm_gain, w_gate, w_up, w_down, expert_ids, slot_ids, route_weights)
+    nz, nx, npair = (lax.axis_size(name) for name in ("expert", "head", "pair"))
+    rows = resid.shape[0]
+    capacity = 2 * rows * TOPK // (w_gate.shape[0] * nz)
+    dense = (
+        capacity == rows
+        and w_gate.shape[0] == 1
+        and nz == nx * npair
+        and nx == 2
+        and npair == 2
+        and query.shape[1] // HEAD_WIDTH == QUERY_HEADS // KEY_VALUE_HEADS
+        and rows % (16 * nx * npair) == 0
+    )
+    return fused_body(*args) if dense else slotted_body(*args)
+
+
 def solution(mesh):
     return jax.shard_map(
         body,

time: 333 us -> 127 us (0.38); the launches traced: 328 us -> 127 us
  waiting for transfers between devices: 232 us -> 0 us
  Pallas kernels: 0 us -> 116 us
  blocking collectives: 44.6 us -> 0 us
  matrix products: 18.8 us -> 0 us
  between operations: 14 us -> 0.65 us
  starting transfers between devices: 4.82 us -> 0 us
  other arithmetic: 4.17 us -> 0 us
    all_gather x3 -> x0, waiting for transfers between devices: 183 us -> none  [the longest x1 131 us: body(): lax.all_gather(wo, 'expert', axis=1, tiled=True)]
    pallas_call x0 -> x1, Pallas kernels: none -> 116 us  [fused_body(): pl.pallas_call(functools.partial(fused_kernel, nz, nx, npair), out_shape=...]
    all_to_all x1 -> x0, blocking collectives: 27.9 us -> none  [body(): lax.all_to_all(filled.reshape(experts_all, 1, capacity, normed.shape[1]),...]
    reduce_scatter x1 -> x0, waiting for transfers between devices: 25.1 us -> none  [body(): lax.psum_scatter(partial_proj.astype(jnp.bfloat16), ('head', 'pair'), sca...]
    all_to_all x1 -> x0, waiting for transfers between devices: 22.7 us -> none  [body(): lax.all_to_all(expert_out, 'expert', split_axis=1, concat_axis=0, tiled=T...]
    dot_general x7 -> x0, matrix products: 18.8 us -> none  [the longest x1 5.77 us: body(): jnp.dot(heads_out, lax.all_gather(wo, 'expert', axis=1, tiled=True), pref...]
    all_gather x1 -> x0, blocking collectives: 11 us -> none  [body(): shards = lax.all_gather(keyval, 'expert', axis=1, tiled=True)]
    unnamed x24 -> x16, local copies, waits for them, and re-layouts: 1.69 us -> 9.67 us
  transfers between devices with their start and end apart: 5 -> 0, of which waited for: 5 -> 0; matrix products, arithmetic and copies ran while one was open for 3% -> 0% of each run, Pallas kernels for 0% -> 0%
where the time goes in v1:
time: 127 us
  Pallas kernels  116 us (91%)
  local copies, waits for them, and re-layouts  9.67 us (8%)
    pallas_call x1, Pallas kernels, fused_body(): pl.pallas_call(functools.partial(fused_kernel, nz, nx, npair), out_shape=...  116 us
    unnamed x16, local copies, waits for them, and re-layouts  9.67 us

profile of v1, /device:TPU:25, one launch (start us, length us, event | category | flops | bytes accessed | tf_op | source)
XLA Modules:
  0.0 126.7 jit_solution(8885361980153777124)
XLA Ops:
  0.6 0.8 copy.12.ids_ref
  1.4 0.8 copy.13.rw_ref
  2.2 0.0 copy-start
  2.2 1.6 %copy-done = bf16[1024,1024]{1,0:T(8,128)(2,1)S(1)} copy-done((bf16[1024,1024]{1,0:T(8,128)(2,1)S(1)}, bf16[1024,1024]{1,0:T(8,128)(2,1)}, u32[]{:S(2)}) %copy-start) | copy-done | bytes 2097176
  3.8 0.0 copy-start.1
  3.8 1.6 %copy-done.1 = bf16[1,4096,256]{2,1,0:T(8,128)(2,1)S(1)} copy-done((bf16[1,4096,256]{2,1,0:T(8,128)(2,1)S(1)}, bf16[1,4096,256]{2,1,0:T(8,128)(2,1)}, u32[]{:S(2)}) %copy-start.1) | copy-done | bytes 2097176
  5.4 0.0 copy-start.2
  5.4 0.9 copy-done.2
  6.3 0.0 copy-start.3
  6.3 0.9 copy-done.3
  7.3 0.0 copy-start.4
  7.3 0.9 copy-done.4
  8.2 0.0 copy-start.5
  8.2 0.7 copy-done.5
  8.9 116.3 %shard_map.113 = (bf16[128,1024]{1,0:T(8,128)(2,1)S(1)}, bf16[128,1024]{1,0:T(8,128)(2,1)S(1)}) custom-call(bf16[128,1024]{1,0:T(8,128)(2,1)S(1)} %copy-done.2, bf16[2,128,256]{2,1,0:T(8,128)(2,1)S(1)} %copy-done.4, bf16[128,1024]{1,0:T(8,128)(2,1)S(1)} %copy-done.3, f32[4,1,1024]{2,1,0:T(1,128)S(1)} %bitcast.1, s32[128,2]{1,0:T(8,128)S(1)} %copy.12.ids_ref, ...), custom_call_target="tpu_custom_call" | custom-call | flops 4294967296 | bytes 8388608 | tf_op jit(solution)/shard_map/pallas_call | solution.py:386
  125.2 0.7 copy.16
  126.0 0.7 copy.17
Async XLA Ops:
  2.2 1.6 %copy-start = (bf16[1024,1024]{1,0:T(8,128)(2,1)S(1)}, bf16[1024,1024]{1,0:T(8,128)(2,1)}, u32[]{:S(2)}) copy-start(bf16[1024,1024]{1,0:T(8,128)(2,1)} %wo_hbm.1) | copy-start | bytes 6291460
  3.8 1.6 %copy-start.1 = (bf16[1,4096,256]{2,1,0:T(8,128)(2,1)S(1)}, bf16[1,4096,256]{2,1,0:T(8,128)(2,1)}, u32[]{:S(2)}) copy-start(bf16[1,4096,256]{2,1,0:T(8,128)(2,1)} %wg_hbm.1) | copy-start | bytes 6291460
  5.4 0.9 copy-start.2
  6.3 0.9 copy-start.3
  7.3 0.9 copy-start.4
  8.2 0.7 copy-start.5

commit v2 on v1

--- a/solution.py
+++ b/solution.py
@@ -119,10 +119,11 @@
 
 
 def fused_kernel(
-    nz, nx, npair, q_ref, kv_ref, resid_ref, gain_ref, ids_ref, rw_ref, wo_hbm, wg_hbm, wu_hbm, wd_hbm,
+    nz, nx, npair, q_hbm, kv_hbm, resid_hbm, gain_hbm, ids_hbm, rw_hbm, wo_hbm, wg_hbm, wu_hbm, wd_hbm,
     hid_ref, mix_ref,
+    q_ref, gain_ref, ids_ref, rw_ref,
     wo, wgu, wd, kv_all, ho, pbuf, pin, resid_t, xall, act_all, eo, ret,
-    w_sem, self_sem, kv_s, kv_r, rs_s, rs_r, ho_s, ho_r, p_s, p_r, z_s, z_r, x_s, x_r, c_s, c_r, f_s, f_r,
+    w_sem, in_sem, kv_s, kv_r, rs_s, rs_r, ho_s, ho_r, p_s, p_r, z_s, z_r, x_s, x_r, c_s, c_r, f_s, f_r,
     a_s, a_r, e_s, e_r,
 ):
     nhp = nx * npair
@@ -133,6 +134,7 @@
     part_rows = rows // nhp
     hidden = wg_hbm.shape[2]
     heads = cols // HEAD_WIDTH
+    half = cols // 2
     f32, bf16 = jnp.float32, jnp.bfloat16
 
     def at(zt, hpt):
@@ -143,27 +145,39 @@
             src_ref=src, dst_ref=dst, send_sem=ssem, recv_sem=rsem, device_id=dev, device_id_type=MESH
         )
 
+    def same(ref, ssem, rsem, dev):
+        return remote(ref, ref, ssem, rsem, dev)
+
     def slab(index):
         return pl.ds(pl.multiple_of(index * part_rows, part_rows), part_rows)
 
     mine = slab(hp)
     z_others = [lax.rem(z + d, nz) for d in range(1, nz)]
     hp_others = [lax.rem(hp + d, nhp) for d in range(1, nhp)]
+    right_ok, left_ok = z + 1 < nz, z > 0
+    right, left = lax.rem(z + 1, nz), lax.rem(z + nz - 1, nz)
     x_dev = (g, z, 1 - x, p)
     c_dev = (g, z, x, 1 - p)
     hp_x = (1 - x) * npair + p
     hp_c = x * npair + 1 - p
     hp_xc = (1 - x) * npair + 1 - p
 
+    key_cols = pl.ds(pl.multiple_of(p * HEAD_WIDTH, HEAD_WIDTH), HEAD_WIDTH)
+    small = [
+        pltpu.make_async_copy(kv_hbm.at[:, :, key_cols], kv_all.at[z], in_sem.at[0]),
+        pltpu.make_async_copy(q_hbm, q_ref, in_sem.at[1]),
+        pltpu.make_async_copy(gain_hbm, gain_ref, in_sem.at[2]),
+        pltpu.make_async_copy(ids_hbm, ids_ref, in_sem.at[3]),
+        pltpu.make_async_copy(rw_hbm, rw_ref, in_sem.at[4]),
+    ]
     weights = [
         pltpu.make_async_copy(wo_hbm, wo, w_sem.at[0]),
         pltpu.make_async_copy(wg_hbm.at[0], wgu.at[:, 0:hidden], w_sem.at[1]),
         pltpu.make_async_copy(wu_hbm.at[0], wgu.at[:, hidden : 2 * hidden], w_sem.at[2]),
         pltpu.make_async_copy(wd_hbm.at[0], wd, w_sem.at[3]),
     ]
-    for copy in weights:
+    for copy in small + weights:
         copy.start()
-    kv_all[z] = kv_ref[:, :, pl.ds(pl.multiple_of(p * HEAD_WIDTH, HEAD_WIDTH), HEAD_WIDTH)]
 
     barrier = pltpu.get_barrier_semaphore()
     for dz in range(nz):
@@ -177,17 +191,19 @@
                 )
     pl.semaphore_wait(barrier, nz * nhp - 1)
 
-    def kv_copy(i, zt):
-        return remote(kv_all.at[z], kv_all.at[z], kv_s.at[i], kv_r.at[z], at(zt, hp))
-
-    for d in range(nz - 1, 0, -1):
-        @pl.when(z + d < nz)
-        def _():
-            kv_copy(d, lax.rem(z + d, nz)).start()
+    def kv_copy(b):
+        return same(kv_all.at[b], kv_s.at[b], kv_r.at[b], at(right, hp))
+
+    small[0].wait()
+
+    @pl.when(right_ok)
+    def _():
+        kv_copy(z).start()
 
     def resid_copy(j):
-        return remote(resid_ref.at[pl.ds(j * part_rows, part_rows)], resid_t.at[z], rs_s.at[j], rs_r.at[z], at(hp, j))
-
+        return remote(resid_hbm.at[pl.ds(j * part_rows, part_rows)], resid_t.at[z], rs_s.at[j], rs_r.at[z], at(hp, j))
+
+    own_resid = pltpu.make_async_copy(resid_hbm.at[mine], resid_t.at[z], in_sem.at[5])
     for j in range(nhp):
         is_self = jnp.logical_and(z == hp, hp == j)
 
@@ -195,16 +211,25 @@
         def _():
             resid_copy(j).start()
 
-        @pl.when(is_self)
-        def _():
-            resid_t[z] = resid_ref[pl.ds(j * part_rows, part_rows), :]
+    @pl.when(z == hp)
+    def _():
+        own_resid.start()
+
+    for copy in small[1:]:
+        copy.wait()
+
+    def ho_copy(b, part, way, dev):
+        ref = ho.at[b, :, part * half : (part + 1) * half]
+        return same(ref, ho_s.at[b, part, way], ho_r.at[b, part], at(dev, hp))
 
     scale = 1.0 / math.sqrt(HEAD_WIDTH)
     for n in range(nz):
         @pl.when(z == n)
         def _():
-            for b in range(n):
-                remote(kv_all.at[b], kv_all.at[b], kv_s.at[0], kv_r.at[b], at(b, hp)).wait_recv()
+            for b in range(n - 1, -1, -1):
+                kv_copy(b).wait_recv()
+                if n + 1 < nz:
+                    kv_copy(b).start()
             count = (n + 1) * rows
             keys = kv_all[0 : n + 1, 0].reshape(count, HEAD_WIDTH)
             values = kv_all[0 : n + 1, 1].reshape(count, HEAD_WIDTH)
@@ -221,25 +246,27 @@
                 total = jnp.sum(probs, axis=1, keepdims=True)
                 mixed = jnp.dot(probs.astype(bf16), values, preferred_element_type=f32)
                 ho[n, :, span] = (mixed / total).astype(bf16)
-
-    def ho_copy(i):
-        return remote(ho.at[z], ho.at[z], ho_s.at[i], ho_r.at[z], at(z_others[i], hp))
-
-    for i in range(nz - 1):
-        ho_copy(i).start()
-    weights[0].wait()
+                if h % (heads // 2) == heads // 2 - 1:
+                    part = h // (heads // 2)
+                    if n + 1 < nz:
+                        ho_copy(n, part, 0, n + 1).start()
+                    if n > 0:
+                        ho_copy(n, part, 1, n - 1).start()
 
     def p_copy(b, i):
         return remote(pbuf.at[b, slab(hp_others[i])], pin.at[b, hp], p_s.at[b, i], p_r.at[b, hp], at(z, hp_others[i]))
 
-    def z_copy(b, i):
-        return remote(
-            xall.at[b, z, mine], xall.at[b, z, mine], z_s.at[b, i], z_r.at[b, z], at(z_others[i], hp)
-        )
-
-    def group_copy(b, owner, ssem, rsem, dev):
-        ref = xall.at[b, :, slab(owner)]
-        return remote(ref, ref, ssem.at[b], rsem.at[b], dev)
+    def z_copy(b, e, way, dev):
+        return same(xall.at[b, e, mine], z_s.at[b, e, way], z_r.at[b, e], at(dev, hp))
+
+    def x_copy(b, e, owner):
+        return same(xall.at[b, e, slab(owner)], x_s.at[b, e], x_r.at[b, e], x_dev)
+
+    def c_copy(b, e, owner):
+        return same(xall.at[b, e, slab(owner)], c_s.at[b, e], c_r.at[b, e], c_dev)
+
+    def f_copy(b, e, owner):
+        return same(xall.at[b, e, slab(owner)], f_s.at[b, e], f_r.at[b, e], c_dev)
 
     def a_copy(b, i):
         return remote(act_all.at[b, hp], act_all.at[b, hp], a_s.at[b, i], a_r.at[b, hp], at(z, hp_others[i]))
@@ -248,20 +275,46 @@
         return remote(eo.at[b], ret.at[z], e_s.at[b], e_r.at[z], at(b, hp))
 
     def project(b):
-        @pl.when(z != b)
-        def _():
-            remote(ho.at[b], ho.at[b], ho_s.at[0], ho_r.at[b], at(b, hp)).wait_recv()
-
         pbuf[b] = jnp.dot(ho[b], wo[...], preferred_element_type=f32).astype(bf16)
         for i in range(nhp - 1):
             p_copy(b, i).start()
 
+    def heads_hop(d):
+        for part in range(2):
+            @pl.when(z >= d)
+            def _():
+                ho_copy(z - d, part, 0, right).wait_recv()
+
+            @pl.when(jnp.logical_and(z >= d, right_ok))
+            def _():
+                ho_copy(z - d, part, 0, right).start()
+
+            @pl.when(z + d < nz)
+            def _():
+                ho_copy(z + d, part, 1, left).wait_recv()
+
+            @pl.when(jnp.logical_and(z + d < nz, left_ok))
+            def _():
+                ho_copy(z + d, part, 1, left).start()
+
+        @pl.when(z >= d)
+        def _():
+            project(z - d)
+
+        @pl.when(z + d < nz)
+        def _():
+            project(z + d)
+
     def add_up(b):
         @pl.when(jnp.logical_not(jnp.logical_and(z == b, hp == z)))
         def _():
             remote(
-                resid_ref.at[pl.ds(0, part_rows)], resid_t.at[b], rs_s.at[0], rs_r.at[b], at(b, z)
+                resid_hbm.at[pl.ds(0, part_rows)], resid_t.at[b], rs_s.at[0], rs_r.at[b], at(b, z)
             ).wait_recv()
+
+        @pl.when(jnp.logical_and(z == b, hp == z))
+        def _():
+            own_resid.wait()
 
         for other in hp_others:
             remote(pbuf.at[b, mine], pin.at[b, other], p_s.at[b, 0], p_r.at[b, other], at(z, other)).wait_recv()
@@ -269,21 +322,54 @@
         for other in hp_others:
             total = total + pin[b, other].astype(f32)
         xall[b, z, mine, :] = (resid_t[b].astype(f32) + total).astype(bf16)
-        for i in range(nz - 1):
-            z_copy(b, i).start()
-
-    def spread(b):
-        for other in z_others:
-            ref = xall.at[b, other, mine]
-            remote(ref, ref, z_s.at[b, 0], z_r.at[b, other], at(other, hp)).wait_recv()
-        group_copy(b, hp, x_s, x_r, x_dev).start()
-        group_copy(b, hp, c_s, c_r, c_dev).start()
+
+        @pl.when(right_ok)
+        def _():
+            z_copy(b, z, 0, right).start()
+
+        @pl.when(left_ok)
+        def _():
+            z_copy(b, z, 1, left).start()
+
+        x_copy(b, z, hp).start()
+        c_copy(b, z, hp).start()
+
+    def spread(b, d):
+        @pl.when(z >= d)
+        def _():
+            z_copy(b, z - d, 0, right).wait_recv()
+
+        @pl.when(jnp.logical_and(z >= d, right_ok))
+        def _():
+            z_copy(b, z - d, 0, right).start()
+
+        @pl.when(z + d < nz)
+        def _():
+            z_copy(b, z + d, 1, left).wait_recv()
+
+        @pl.when(jnp.logical_and(z + d < nz, left_ok))
+        def _():
+            z_copy(b, z + d, 1, left).start()
+
+        @pl.when(z >= d)
+        def _():
+            x_copy(b, z - d, hp).start()
+            c_copy(b, z - d, hp).start()
+
+        @pl.when(z + d < nz)
+        def _():
+            x_copy(b, z + d, hp).start()
+            c_copy(b, z + d, hp).start()
+
+    def pass_on(b):
+        for e in range(nz):
+            x_copy(b, e, hp_x).wait_recv()
+            f_copy(b, e, hp_x).start()
 
     def hidden_units(b):
-        group_copy(b, hp_x, x_s, x_r, x_dev).wait_recv()
-        group_copy(b, hp_x, f_s, f_r, c_dev).start()
-        group_copy(b, hp_c, c_s, c_r, c_dev).wait_recv()
-        group_copy(b, hp_xc, f_s, f_r, c_dev).wait_recv()
+        for e in range(nz):
+            c_copy(b, e, hp_c).wait_recv()
+            f_copy(b, e, hp_xc).wait_recv()
         square = jnp.zeros((rows, 1), f32)
         for e in range(nz):
             part = xall[b, e].astype(f32)
@@ -313,59 +399,89 @@
         def _():
             e_copy(b).start()
 
-    for step in range(nz + 4):
-        if step < nz:
-            project(step)
-        if 0 <= step - 1 < nz:
-            add_up(step - 1)
-        if 0 <= step - 2 < nz:
-            spread(step - 2)
-        if 0 <= step - 3 < nz:
-            if step == 3:
-                weights[1].wait()
-                weights[2].wait()
-            hidden_units(step - 3)
-        if 0 <= step - 4 < nz:
-            if step == 4:
-                weights[3].wait()
-            down(step - 4)
+    order = sorted(range(nz), key=lambda b: max(b, nz - 1 - b))
+    first, last = order[: nz // 2], order[nz // 2 :]
+    weights[0].wait()
+    project(z)
+    for d in range(1, nz - 1):
+        heads_hop(d)
+    for b in first:
+        add_up(b)
+    heads_hop(nz - 1)
+    for b in first:
+        spread(b, 1)
+    for b in last:
+        add_up(b)
+    for d in range(2, nz):
+        for b in first:
+            spread(b, d)
+        for b in last:
+            spread(b, d - 1)
+    pass_on(first[0])
+    for b in last:
+        spread(b, nz - 1)
+    weights[1].wait()
+    weights[2].wait()
+    weights[3].wait()
+    for i in range(nz + 1):
+        if i + 1 < nz:
+            pass_on(order[i + 1])
+        if i < nz:
+            hidden_units(order[i])
+        if i >= 1:
+            down(order[i - 1])
 
     hid_ref[...] = xall[z, hp]
-    mix = route_share(ids_ref, rw_ref, z) * eo[z].astype(f32)
+    diagonal = lax.broadcasted_iota(jnp.int32, (rows, rows), 0) == lax.broadcasted_iota(
+        jnp.int32, (rows, rows), 1
+    )
+
+    def route_share(expert):
+        shares = jnp.sum(jnp.where(ids_ref[...] == expert, rw_ref[...], 0.0), axis=0, keepdims=True)
+        return jnp.sum(jnp.where(diagonal, shares, 0.0), axis=1, keepdims=True)
+
+    mix = route_share(z) * eo[z].astype(f32)
     for other in z_others:
         remote(eo.at[0], ret.at[other], e_s.at[0], e_r.at[other], at(other, hp)).wait_recv()
-        mix = mix + route_share(ids_ref, rw_ref, other) * ret[other].astype(f32)
+        mix = mix + route_share(other) * ret[other].astype(f32)
     mix_ref[...] = mix.astype(bf16)
-
-    for d in range(1, nz):
-        @pl.when(z + d < nz)
-        def _():
-            kv_copy(d, lax.rem(z + d, nz)).wait_send()
 
     for j in range(nhp):
         @pl.when(jnp.logical_not(jnp.logical_and(z == hp, hp == j)))
         def _():
             resid_copy(j).wait_send()
 
-    for i in range(nz - 1):
-        ho_copy(i).wait_send()
     for b in range(nz):
+        @pl.when(jnp.logical_and(z >= b, right_ok))
+        def _():
+            kv_copy(b).wait_send()
+            for part in range(2):
+                ho_copy(b, part, 0, right).wait_send()
+
+        @pl.when(jnp.logical_and(z <= b, left_ok))
+        def _():
+            for part in range(2):
+                ho_copy(b, part, 1, left).wait_send()
+
         for i in range(nhp - 1):
             p_copy(b, i).wait_send()
             a_copy(b, i).wait_send()
-        for i in range(nz - 1):
-            z_copy(b, i).wait_send()
-        group_copy(b, hp, x_s, x_r, x_dev).wait_send()
-        group_copy(b, hp, c_s, c_r, c_dev).wait_send()
-        group_copy(b, hp_x, f_s, f_r, c_dev).wait_send()
+        for e in range(nz):
+            @pl.when(jnp.logical_and(z >= e, right_ok))
+            def _():
+                z_copy(b, e, 0, right).wait_send()
+
+            @pl.when(jnp.logical_and(z <= e, left_ok))
+            def _():
+                z_copy(b, e, 1, left).wait_send()
+
+            x_copy(b, e, hp).wait_send()
+            c_copy(b, e, hp).wait_send()
+            f_copy(b, e, hp_x).wait_send()
 
         @pl.when(z != b)
         def _():
             e_copy(b).wait_send()
-
-
-def route_share(ids_ref, rw_ref, expert):
-    return jnp.sum(jnp.where(ids_ref[...] == expert, rw_ref[...], 0.0), axis=1, keepdims=True)
 
 
 def fused_body(
@@ -386,9 +502,13 @@
     return pl.pallas_call(
         functools.partial(fused_kernel, nz, nx, npair),
         out_shape=(out, out),
-        in_specs=[vmem] * 6 + [anywhere] * 4,
+        in_specs=[anywhere] * 10,
         out_specs=(vmem, vmem),
         scratch_shapes=[
+            pltpu.VMEM((rows, cols), bf16),
+            pltpu.VMEM((nz, 1, cols), jnp.float32),
+            pltpu.VMEM((TOPK, rows), jnp.int32),
+            pltpu.VMEM((TOPK, rows), jnp.float32),
             pltpu.VMEM(wo.shape, bf16),
             pltpu.VMEM((w_gate.shape[1], 2 * hidden), bf16),
             pltpu.VMEM(w_down.shape[1:], bf16),
@@ -402,26 +522,26 @@
             pltpu.VMEM((nz, rows, cols), bf16),
             pltpu.VMEM((nz, rows, cols), bf16),
             dma((4,)),
-            dma((1,)),
+            dma((6,)),
             dma((nz,)), dma((nz,)),
             dma((nhp,)), dma((nz,)),
-            dma((nz,)), dma((nz,)),
+            dma((nz, 2, 2)), dma((nz, 2)),
             dma((nz, nhp)), dma((nz, nhp)),
+            dma((nz, nz, 2)), dma((nz, nz)),
             dma((nz, nz)), dma((nz, nz)),
-            dma((nz,)), dma((nz,)),
-            dma((nz,)), dma((nz,)),
-            dma((nz,)), dma((nz,)),
+            dma((nz, nz)), dma((nz, nz)),
+            dma((nz, nz)), dma((nz, nz)),
             dma((nz, nhp)), dma((nz, nhp)),
             dma((nz,)), dma((nz,)),
         ],
         compiler_params=pltpu.CompilerParams(
-            collective_id=0, has_side_effects=True, vmem_limit_bytes=48 * 1024 * 1024
+            collective_id=0, has_side_effects=True, vmem_limit_bytes=60 * 1024 * 1024
         ),
         cost_estimate=pl.CostEstimate(
             flops=flops, bytes_accessed=2 * (wo.size + 3 * w_gate.size), transcendentals=0
         ),
     )(
-        query, keyval, resid, norm_gain.reshape(nz, 1, cols), expert_ids, route_weights, wo, w_gate, w_up, w_down
+        query, keyval, resid, norm_gain.reshape(nz, 1, cols), expert_ids.T, route_weights.T, wo, w_gate, w_up, w_down
     )
 
 

time: 127 us -> 102 us (0.80)
  Pallas kernels: 116 us -> 97.6 us
  local copies, waits for them, and re-layouts: 9.67 us -> 3.34 us
    pallas_call x1, Pallas kernels: 116 us -> 97.6 us  [fused_body(): pl.pallas_call(functools.partial(fused_kernel, nz, nx, npair), out_shape=...]
    unnamed x16 -> x2, local copies, waits for them, and re-layouts: 9.67 us -> 3.34 us
where the time goes in v2:
time: 102 us
  Pallas kernels  97.6 us (96%)
  local copies, waits for them, and re-layouts  3.34 us (3%)
    pallas_call x1, Pallas kernels, fused_body(): pl.pallas_call(functools.partial(fused_kernel, nz, nx, npair), out_shape=...  97.6 us
    unnamed x2, local copies, waits for them, and re-layouts  3.34 us

profile of v2, /device:TPU:25, one launch (start us, length us, event | category | flops | bytes accessed | tf_op | source)
XLA Modules:
  0.0 101.6 jit_solution(13194443772095142934)
XLA Ops:
  0.6 97.6 %shard_map.113 = (bf16[128,1024]{1,0:T(8,128)(2,1)}, bf16[128,1024]{1,0:T(8,128)(2,1)}) custom-call(bf16[128,1024]{1,0:T(8,128)(2,1)} %q_hbm.1, bf16[2,128,256]{2,1,0:T(8,128)(2,1)} %kv_hbm.1, bf16[128,1024]{1,0:T(8,128)(2,1)} %resid_hbm.1, f32[4,1,1024]{2,1,0:T(1,128)} %bitcast.3, s32[2,128]{1,0:T(2,128)} %bitcast.4, f32[2,128]{1,0:T(2,128)} %bitcast.5, ...), custom_call_target="tpu_custom_call" | custom-call | flops 4294967296 | bytes 8388608 | tf_op jit(solution)/shard_map/pallas_call | solution.py:502
  98.2 1.7 %copy.14 = bf16[128,1024]{1,0:T(8,128)(2,1)} copy(bf16[128,1024]{1,0:T(8,128)(2,1)} %get-tuple-element.4) | data formatting | bytes 524288
  99.9 1.7 %copy.15 = bf16[128,1024]{1,0:T(8,128)(2,1)} copy(bf16[128,1024]{1,0:T(8,128)(2,1)} %get-tuple-element.5) | data formatting | bytes 524288

commit v3 on v2

--- a/solution.py
+++ b/solution.py
@@ -121,16 +121,16 @@
 def fused_kernel(
     nz, nx, npair, q_hbm, kv_hbm, resid_hbm, gain_hbm, ids_hbm, rw_hbm, wo_hbm, wg_hbm, wu_hbm, wd_hbm,
     hid_ref, mix_ref,
-    q_ref, gain_ref, ids_ref, rw_ref,
-    wo, wgu, wd, kv_all, ho, pbuf, pin, resid_t, xall, act_all, eo, ret,
-    w_sem, in_sem, kv_s, kv_r, rs_s, rs_r, ho_s, ho_r, p_s, p_r, z_s, z_r, x_s, x_r, c_s, c_r, f_s, f_r,
+    gain_ref, ids_ref, rw_ref,
+    wo, wgu, wd, kv_all, q_all, ho, pbuf, pin, resid_s, resid_t, xall, act_all, eo, ret,
+    w_sem, in_sem, kv_s, kv_r, rs_s, rs_r, rt_s, rt_r, q_s, q_r, p_s, p_r, z_s, z_r, x_s, x_r, c_s, c_r, f_s, f_r,
     a_s, a_r, e_s, e_r,
 ):
     nhp = nx * npair
     g, z = lax.axis_index("groups"), lax.axis_index("expert")
     x, p = lax.axis_index("head"), lax.axis_index("pair")
     hp = x * npair + p
-    rows, cols = q_ref.shape
+    rows, cols = q_hbm.shape
     part_rows = rows // nhp
     hidden = wg_hbm.shape[2]
     heads = cols // HEAD_WIDTH
@@ -165,7 +165,7 @@
     key_cols = pl.ds(pl.multiple_of(p * HEAD_WIDTH, HEAD_WIDTH), HEAD_WIDTH)
     small = [
         pltpu.make_async_copy(kv_hbm.at[:, :, key_cols], kv_all.at[z], in_sem.at[0]),
-        pltpu.make_async_copy(q_hbm, q_ref, in_sem.at[1]),
+        pltpu.make_async_copy(q_hbm, q_all.at[z], in_sem.at[1]),
         pltpu.make_async_copy(gain_hbm, gain_ref, in_sem.at[2]),
         pltpu.make_async_copy(ids_hbm, ids_ref, in_sem.at[3]),
         pltpu.make_async_copy(rw_hbm, rw_ref, in_sem.at[4]),
@@ -191,67 +191,76 @@
                 )
     pl.semaphore_wait(barrier, nz * nhp - 1)
 
-    def kv_copy(b):
-        return same(kv_all.at[b], kv_s.at[b], kv_r.at[b], at(right, hp))
-
-    small[0].wait()
-
-    @pl.when(right_ok)
-    def _():
-        kv_copy(z).start()
-
-    def resid_copy(j):
-        return remote(resid_hbm.at[pl.ds(j * part_rows, part_rows)], resid_t.at[z], rs_s.at[j], rs_r.at[z], at(hp, j))
-
-    own_resid = pltpu.make_async_copy(resid_hbm.at[mine], resid_t.at[z], in_sem.at[5])
-    for j in range(nhp):
-        is_self = jnp.logical_and(z == hp, hp == j)
-
-        @pl.when(jnp.logical_not(is_self))
-        def _():
-            resid_copy(j).start()
-
-    @pl.when(z == hp)
-    def _():
-        own_resid.start()
-
-    for copy in small[1:]:
+    def kv_copy(i):
+        return remote(kv_hbm.at[:, :, key_cols], kv_all.at[z], kv_s.at[i], kv_r.at[z], at(z_others[i], hp))
+
+    for i in range(nz - 1):
+        kv_copy(i).start()
+
+    def q_copy(b, part, way, dev):
+        ref = q_all.at[b, :, part * half : (part + 1) * half]
+        return same(ref, q_s.at[b, part, way], q_r.at[b, part], at(dev, hp))
+
+    def q_own(part, way, dev):
+        span = slice(part * half, (part + 1) * half)
+        return remote(
+            q_hbm.at[:, span], q_all.at[z, :, span], q_s.at[z, part, way], q_r.at[z, part], at(dev, hp)
+        )
+
+    for part in range(2):
+        @pl.when(right_ok)
+        def _():
+            q_own(part, 0, right).start()
+
+        @pl.when(left_ok)
+        def _():
+            q_own(part, 1, left).start()
+
+    def resid_copy(i):
+        return remote(resid_hbm.at[slab(hp_others[i])], resid_s.at[hp], rs_s.at[i], rs_r.at[hp], at(z, hp_others[i]))
+
+    def resid_wait(j):
+        return remote(resid_hbm.at[mine], resid_s.at[j], rs_s.at[0], rs_r.at[j], at(z, j))
+
+    def resid_along(i):
+        return remote(resid_s.at[z_others[i]], resid_t.at[z], rt_s.at[i], rt_r.at[z], at(z_others[i], hp))
+
+    own_resid = pltpu.make_async_copy(resid_hbm.at[mine], resid_s.at[hp], in_sem.at[5])
+    own_resid.start()
+    for i in range(nhp - 1):
+        resid_copy(i).start()
+    own_resid.wait()
+    for other in hp_others:
+        resid_wait(other).wait_recv()
+    for i in range(nz - 1):
+        resid_along(i).start()
+    resid_t[z] = resid_s[z]
+
+    for copy in small:
         copy.wait()
 
-    def ho_copy(b, part, way, dev):
-        ref = ho.at[b, :, part * half : (part + 1) * half]
-        return same(ref, ho_s.at[b, part, way], ho_r.at[b, part], at(dev, hp))
-
     scale = 1.0 / math.sqrt(HEAD_WIDTH)
-    for n in range(nz):
-        @pl.when(z == n)
-        def _():
-            for b in range(n - 1, -1, -1):
-                kv_copy(b).wait_recv()
-                if n + 1 < nz:
-                    kv_copy(b).start()
-            count = (n + 1) * rows
-            keys = kv_all[0 : n + 1, 0].reshape(count, HEAD_WIDTH)
-            values = kv_all[0 : n + 1, 1].reshape(count, HEAD_WIDTH)
-            row = lax.broadcasted_iota(jnp.int32, (rows, count), 0) + n * rows
-            col = lax.broadcasted_iota(jnp.int32, (rows, count), 1)
-            visible = col <= row
-            for h in range(heads):
-                span = slice(h * HEAD_WIDTH, (h + 1) * HEAD_WIDTH)
-                scores = lax.dot_general(
-                    q_ref[:, span], keys, (((1,), (1,)), ((), ())), preferred_element_type=f32
-                )
-                scores = jnp.where(visible, scores * scale, -jnp.inf)
-                probs = jnp.exp(scores - jnp.max(scores, axis=1, keepdims=True))
-                total = jnp.sum(probs, axis=1, keepdims=True)
-                mixed = jnp.dot(probs.astype(bf16), values, preferred_element_type=f32)
-                ho[n, :, span] = (mixed / total).astype(bf16)
-                if h % (heads // 2) == heads // 2 - 1:
-                    part = h // (heads // 2)
-                    if n + 1 < nz:
-                        ho_copy(n, part, 0, n + 1).start()
-                    if n > 0:
-                        ho_copy(n, part, 1, n - 1).start()
+    lower = lax.broadcasted_iota(jnp.int32, (rows, rows), 1) <= lax.broadcasted_iota(
+        jnp.int32, (rows, rows), 0
+    )
+
+    def attend(b):
+        count = (b + 1) * rows
+        keys = kv_all[0 : b + 1, 0].reshape(count, HEAD_WIDTH)
+        values = kv_all[0 : b + 1, 1].reshape(count, HEAD_WIDTH)
+        for h in range(heads):
+            span = slice(h * HEAD_WIDTH, (h + 1) * HEAD_WIDTH)
+            scores = lax.dot_general(
+                q_all[b, :, span], keys, (((1,), (1,)), ((), ())), preferred_element_type=f32
+            )
+            scores = scores * scale
+            kept = jnp.where(lower, scores[:, b * rows :], -jnp.inf)
+            if b:
+                kept = jnp.concatenate([scores[:, : b * rows], kept], axis=1)
+            probs = jnp.exp(kept - jnp.max(kept, axis=1, keepdims=True))
+            total = jnp.sum(probs, axis=1, keepdims=True)
+            mixed = jnp.dot(probs.astype(bf16), values, preferred_element_type=f32)
+            ho[b, :, span] = (mixed / total).astype(bf16)
 
     def p_copy(b, i):
         return remote(pbuf.at[b, slab(hp_others[i])], pin.at[b, hp], p_s.at[b, i], p_r.at[b, hp], at(z, hp_others[i]))
@@ -279,42 +288,28 @@
         for i in range(nhp - 1):
             p_copy(b, i).start()
 
-    def heads_hop(d):
+    def query_hop(d):
         for part in range(2):
             @pl.when(z >= d)
             def _():
-                ho_copy(z - d, part, 0, right).wait_recv()
+                q_copy(z - d, part, 0, right).wait_recv()
 
             @pl.when(jnp.logical_and(z >= d, right_ok))
             def _():
-                ho_copy(z - d, part, 0, right).start()
+                q_copy(z - d, part, 0, right).start()
 
             @pl.when(z + d < nz)
             def _():
-                ho_copy(z + d, part, 1, left).wait_recv()
+                q_copy(z + d, part, 1, left).wait_recv()
 
             @pl.when(jnp.logical_and(z + d < nz, left_ok))
             def _():
-                ho_copy(z + d, part, 1, left).start()
-
-        @pl.when(z >= d)
-        def _():
-            project(z - d)
-
-        @pl.when(z + d < nz)
-        def _():
-            project(z + d)
+                q_copy(z + d, part, 1, left).start()
 
     def add_up(b):
-        @pl.when(jnp.logical_not(jnp.logical_and(z == b, hp == z)))
-        def _():
-            remote(
-                resid_hbm.at[pl.ds(0, part_rows)], resid_t.at[b], rs_s.at[0], rs_r.at[b], at(b, z)
-            ).wait_recv()
-
-        @pl.when(jnp.logical_and(z == b, hp == z))
-        def _():
-            own_resid.wait()
+        @pl.when(z != b)
+        def _():
+            remote(resid_s.at[0], resid_t.at[b], rt_s.at[0], rt_r.at[b], at(b, hp)).wait_recv()
 
         for other in hp_others:
             remote(pbuf.at[b, mine], pin.at[b, other], p_s.at[b, 0], p_r.at[b, other], at(z, other)).wait_recv()
@@ -401,22 +396,52 @@
 
     order = sorted(range(nz), key=lambda b: max(b, nz - 1 - b))
     first, last = order[: nz // 2], order[nz // 2 :]
+    query_hop(1)
+    for other in z_others:
+        remote(kv_hbm.at[:, :, key_cols], kv_all.at[other], kv_s.at[0], kv_r.at[other], at(other, hp)).wait_recv()
     weights[0].wait()
-    project(z)
-    for d in range(1, nz - 1):
-        heads_hop(d)
+    near_first = z < nz // 2
+
+    @pl.when(near_first)
+    def _():
+        attend(first[0])
+
+    @pl.when(jnp.logical_not(near_first))
+    def _():
+        attend(first[1])
+
+    for d in range(2, nz - 1):
+        query_hop(d)
+
+    @pl.when(near_first)
+    def _():
+        attend(first[1])
+
+    @pl.when(jnp.logical_not(near_first))
+    def _():
+        attend(first[0])
+
+    for b in first:
+        project(b)
     for b in first:
         add_up(b)
-    heads_hop(nz - 1)
+    query_hop(nz - 1)
+    attend(last[0])
+    project(last[0])
     for b in first:
         spread(b, 1)
+    attend(last[1])
+    project(last[1])
+    add_up(last[0])
+    for b in first:
+        spread(b, 2)
+    add_up(last[1])
+    spread(last[0], 1)
+    for b in first:
+        spread(b, 3)
+    spread(last[1], 1)
     for b in last:
-        add_up(b)
-    for d in range(2, nz):
-        for b in first:
-            spread(b, d)
-        for b in last:
-            spread(b, d - 1)
+        spread(b, 2)
     pass_on(first[0])
     for b in last:
         spread(b, nz - 1)
@@ -446,22 +471,20 @@
         mix = mix + route_share(other) * ret[other].astype(f32)
     mix_ref[...] = mix.astype(bf16)
 
-    for j in range(nhp):
-        @pl.when(jnp.logical_not(jnp.logical_and(z == hp, hp == j)))
-        def _():
-            resid_copy(j).wait_send()
-
+    for i in range(nhp - 1):
+        resid_copy(i).wait_send()
+    for i in range(nz - 1):
+        resid_along(i).wait_send()
+        kv_copy(i).wait_send()
     for b in range(nz):
-        @pl.when(jnp.logical_and(z >= b, right_ok))
-        def _():
-            kv_copy(b).wait_send()
-            for part in range(2):
-                ho_copy(b, part, 0, right).wait_send()
-
-        @pl.when(jnp.logical_and(z <= b, left_ok))
-        def _():
-            for part in range(2):
-                ho_copy(b, part, 1, left).wait_send()
+        for part in range(2):
+            @pl.when(jnp.logical_and(z >= b, right_ok))
+            def _():
+                q_copy(b, part, 0, right).wait_send()
+
+            @pl.when(jnp.logical_and(z <= b, left_ok))
+            def _():
+                q_copy(b, part, 1, left).wait_send()
 
         for i in range(nhp - 1):
             p_copy(b, i).wait_send()
@@ -495,17 +518,16 @@
     bf16 = jnp.bfloat16
     dma = pltpu.SemaphoreType.DMA
     vmem = pl.BlockSpec(memory_space=pltpu.VMEM)
-    anywhere = pl.BlockSpec(memory_space=pl.ANY)
+    in_hbm = pl.BlockSpec(memory_space=pl.ANY)
     out = jax.ShapeDtypeStruct((rows, cols), bf16)
     tokens = nz * rows
     flops = 2 * tokens * (wo.shape[0] * cols + 2 * w_gate.shape[1] * hidden + w_down.shape[1] * cols)
     return pl.pallas_call(
         functools.partial(fused_kernel, nz, nx, npair),
         out_shape=(out, out),
-        in_specs=[anywhere] * 10,
+        in_specs=[in_hbm] * 10,
         out_specs=(vmem, vmem),
         scratch_shapes=[
-            pltpu.VMEM((rows, cols), bf16),
             pltpu.VMEM((nz, 1, cols), jnp.float32),
             pltpu.VMEM((TOPK, rows), jnp.int32),
             pltpu.VMEM((TOPK, rows), jnp.float32),
@@ -515,7 +537,9 @@
             pltpu.VMEM((nz, 2, rows, HEAD_WIDTH), bf16),
             pltpu.VMEM((nz, rows, cols), bf16),
             pltpu.VMEM((nz, rows, cols), bf16),
+            pltpu.VMEM((nz, rows, cols), bf16),
             pltpu.VMEM((nz, nhp, part_rows, cols), bf16),
+            pltpu.VMEM((nhp, part_rows, cols), bf16),
             pltpu.VMEM((nz, part_rows, cols), bf16),
             pltpu.VMEM((nz, nz, rows, cols), bf16),
             pltpu.VMEM((nz, nhp, rows, hidden), bf16),
@@ -524,7 +548,8 @@
             dma((4,)),
             dma((6,)),
             dma((nz,)), dma((nz,)),
-            dma((nhp,)), dma((nz,)),
+            dma((nhp,)), dma((nhp,)),
+            dma((nz,)), dma((nz,)),
             dma((nz, 2, 2)), dma((nz, 2)),
             dma((nz, nhp)), dma((nz, nhp)),
             dma((nz, nz, 2)), dma((nz, nz)),

time: 102 us -> 105 us (1.029)
  Pallas kernels: 97.6 us -> 101 us
    pallas_call x1, Pallas kernels: 97.6 us -> 101 us  [fused_body(): pl.pallas_call(functools.partial(fused_kernel, nz, nx, npair), out_shape=...]
where the time goes in v3:
time: 105 us
  Pallas kernels  101 us (96%)
  local copies, waits for them, and re-layouts  3.34 us (3%)
    pallas_call x1, Pallas kernels, fused_body(): pl.pallas_call(functools.partial(fused_kernel, nz, nx, npair), out_shape=...  101 us
    unnamed x2, local copies, waits for them, and re-layouts  3.34 us

profile of v3, /device:TPU:25, one launch (start us, length us, event | category | flops | bytes accessed | tf_op | source)
XLA Modules:
  0.0 104.7 jit_solution(8190178694960168447)
XLA Ops:
  0.6 100.7 %shard_map.113 = (bf16[128,1024]{1,0:T(8,128)(2,1)}, bf16[128,1024]{1,0:T(8,128)(2,1)}) custom-call(bf16[128,1024]{1,0:T(8,128)(2,1)} %q_hbm.1, bf16[2,128,256]{2,1,0:T(8,128)(2,1)} %kv_hbm.1, bf16[128,1024]{1,0:T(8,128)(2,1)} %resid_hbm.1, f32[4,1,1024]{2,1,0:T(1,128)} %bitcast.3, s32[2,128]{1,0:T(2,128)} %bitcast.4, f32[2,128]{1,0:T(2,128)} %bitcast.5, ...), custom_call_target="tpu_custom_call" | custom-call | flops 4294967296 | bytes 8388608 | tf_op jit(solution)/shard_map/pallas_call | solution.py:525
  101.3 1.7 %copy.14 = bf16[128,1024]{1,0:T(8,128)(2,1)} copy(bf16[128,1024]{1,0:T(8,128)(2,1)} %get-tuple-element.4) | data formatting | bytes 524288
  103.0 1.7 %copy.15 = bf16[128,1024]{1,0:T(8,128)(2,1)} copy(bf16[128,1024]{1,0:T(8,128)(2,1)} %get-tuple-element.5) | data formatting | bytes 524288

commit v4 on v3

--- a/solution.py
+++ b/solution.py
@@ -122,7 +122,7 @@
     nz, nx, npair, q_hbm, kv_hbm, resid_hbm, gain_hbm, ids_hbm, rw_hbm, wo_hbm, wg_hbm, wu_hbm, wd_hbm,
     hid_ref, mix_ref,
     gain_ref, ids_ref, rw_ref,
-    wo, wgu, wd, kv_all, q_all, ho, pbuf, pin, resid_s, resid_t, xall, act_all, eo, ret,
+    wo, wgu, wd, kv_all, q_all, ho, pbuf, psum, pin, resid_s, resid_t, xall, act_all, eo, ret,
     w_sem, in_sem, kv_s, kv_r, rs_s, rs_r, rt_s, rt_r, q_s, q_r, p_s, p_r, z_s, z_r, x_s, x_r, c_s, c_r, f_s, f_r,
     a_s, a_r, e_s, e_r,
 ):
@@ -240,30 +240,35 @@
         copy.wait()
 
     scale = 1.0 / math.sqrt(HEAD_WIDTH)
+    stack = heads // 2
     lower = lax.broadcasted_iota(jnp.int32, (rows, rows), 1) <= lax.broadcasted_iota(
         jnp.int32, (rows, rows), 0
     )
+    lower = jnp.concatenate([lower] * stack, axis=0)
 
     def attend(b):
         count = (b + 1) * rows
         keys = kv_all[0 : b + 1, 0].reshape(count, HEAD_WIDTH)
         values = kv_all[0 : b + 1, 1].reshape(count, HEAD_WIDTH)
-        for h in range(heads):
-            span = slice(h * HEAD_WIDTH, (h + 1) * HEAD_WIDTH)
-            scores = lax.dot_general(
-                q_all[b, :, span], keys, (((1,), (1,)), ((), ())), preferred_element_type=f32
-            )
+        for h in range(0, heads, stack):
+            spans = [slice(i * HEAD_WIDTH, (i + 1) * HEAD_WIDTH) for i in range(h, h + stack)]
+            queries = jnp.concatenate([q_all[b, :, span] for span in spans], axis=0)
+            scores = lax.dot_general(queries, keys, (((1,), (1,)), ((), ())), preferred_element_type=f32)
             scores = scores * scale
             kept = jnp.where(lower, scores[:, b * rows :], -jnp.inf)
             if b:
                 kept = jnp.concatenate([scores[:, : b * rows], kept], axis=1)
             probs = jnp.exp(kept - jnp.max(kept, axis=1, keepdims=True))
             total = jnp.sum(probs, axis=1, keepdims=True)
-            mixed = jnp.dot(probs.astype(bf16), values, preferred_element_type=f32)
-            ho[b, :, span] = (mixed / total).astype(bf16)
-
-    def p_copy(b, i):
-        return remote(pbuf.at[b, slab(hp_others[i])], pin.at[b, hp], p_s.at[b, i], p_r.at[b, hp], at(z, hp_others[i]))
+            mixed = (jnp.dot(probs.astype(bf16), values, preferred_element_type=f32) / total).astype(bf16)
+            for i, span in enumerate(spans):
+                ho[b, :, span] = mixed[i * rows : (i + 1) * rows]
+
+    def p_copy(b, i, owner):
+        return remote(pbuf.at[b, slab(owner)], pin.at[b, i], p_s.at[b, i], p_r.at[b, i], c_dev)
+
+    def px_copy(b):
+        return remote(psum.at[b], pin.at[b, 2], p_s.at[b, 2], p_r.at[b, 2], x_dev)
 
     def z_copy(b, e, way, dev):
         return same(xall.at[b, e, mine], z_s.at[b, e, way], z_r.at[b, e], at(dev, hp))
@@ -277,16 +282,21 @@
     def f_copy(b, e, owner):
         return same(xall.at[b, e, slab(owner)], f_s.at[b, e], f_r.at[b, e], c_dev)
 
-    def a_copy(b, i):
-        return remote(act_all.at[b, hp], act_all.at[b, hp], a_s.at[b, i], a_r.at[b, hp], at(z, hp_others[i]))
+    def a_copy(b, i, owner):
+        return same(act_all.at[b, owner], a_s.at[b, i], a_r.at[b, i], c_dev if i else x_dev)
 
     def e_copy(b):
         return remote(eo.at[b], ret.at[z], e_s.at[b], e_r.at[z], at(b, hp))
 
     def project(b):
         pbuf[b] = jnp.dot(ho[b], wo[...], preferred_element_type=f32).astype(bf16)
-        for i in range(nhp - 1):
-            p_copy(b, i).start()
+        p_copy(b, 0, hp_xc).start()
+        p_copy(b, 1, hp_c).start()
+
+    def pair_sum(b):
+        p_copy(b, 0, hp_xc).wait_recv()
+        psum[b] = (pbuf[b, slab(hp_x), :].astype(f32) + pin[b, 0].astype(f32)).astype(bf16)
+        px_copy(b).start()
 
     def query_hop(d):
         for part in range(2):
@@ -311,11 +321,9 @@
         def _():
             remote(resid_s.at[0], resid_t.at[b], rt_s.at[0], rt_r.at[b], at(b, hp)).wait_recv()
 
-        for other in hp_others:
-            remote(pbuf.at[b, mine], pin.at[b, other], p_s.at[b, 0], p_r.at[b, other], at(z, other)).wait_recv()
-        total = pbuf[b, mine, :].astype(f32)
-        for other in hp_others:
-            total = total + pin[b, other].astype(f32)
+        p_copy(b, 1, hp_c).wait_recv()
+        px_copy(b).wait_recv()
+        total = pbuf[b, mine, :].astype(f32) + pin[b, 1].astype(f32) + pin[b, 2].astype(f32)
         xall[b, z, mine, :] = (resid_t[b].astype(f32) + total).astype(bf16)
 
         @pl.when(right_ok)
@@ -376,13 +384,16 @@
             both = both + jnp.dot(normed, wgu[e * cols : (e + 1) * cols, :], preferred_element_type=f32)
         gate, up = both[:, :hidden], both[:, hidden:]
         act_all[b, hp] = (gate / (1.0 + jnp.exp(-gate)) * up).astype(bf16)
-        for i in range(nhp - 1):
-            a_copy(b, i).start()
+        a_copy(b, 0, hp).start()
+        a_copy(b, 1, hp).start()
+
+    def act_pass(b):
+        a_copy(b, 0, hp_x).wait_recv()
+        a_copy(b, 2, hp_x).start()
 
     def down(b):
-        for other in hp_others:
-            ref = act_all.at[b, other]
-            remote(ref, ref, a_s.at[b, 0], a_r.at[b, other], at(z, other)).wait_recv()
+        a_copy(b, 1, hp_c).wait_recv()
+        a_copy(b, 2, hp_xc).wait_recv()
         total = jnp.zeros((rows, cols), f32)
         for j in range(nhp):
             total = total + jnp.dot(
@@ -424,15 +435,19 @@
     for b in first:
         project(b)
     for b in first:
-        add_up(b)
+        pair_sum(b)
     query_hop(nz - 1)
     attend(last[0])
     project(last[0])
     for b in first:
-        spread(b, 1)
+        add_up(b)
+    pair_sum(last[0])
     attend(last[1])
     project(last[1])
+    for b in first:
+        spread(b, 1)
     add_up(last[0])
+    pair_sum(last[1])
     for b in first:
         spread(b, 2)
     add_up(last[1])
@@ -440,11 +455,11 @@
     for b in first:
         spread(b, 3)
     spread(last[1], 1)
+    spread(last[0], 2)
+    pass_on(first[0])
+    spread(last[1], 2)
     for b in last:
-        spread(b, 2)
-    pass_on(first[0])
-    for b in last:
-        spread(b, nz - 1)
+        spread(b, 3)
     weights[1].wait()
     weights[2].wait()
     weights[3].wait()
@@ -455,6 +470,8 @@
             hidden_units(order[i])
         if i >= 1:
             down(order[i - 1])
+        if i < nz:
+            act_pass(order[i])
 
     hid_ref[...] = xall[z, hp]
     diagonal = lax.broadcasted_iota(jnp.int32, (rows, rows), 0) == lax.broadcasted_iota(
@@ -486,9 +503,12 @@
             def _():
                 q_copy(b, part, 1, left).wait_send()
 
-        for i in range(nhp - 1):
-            p_copy(b, i).wait_send()
-            a_copy(b, i).wait_send()
+        p_copy(b, 0, hp_xc).wait_send()
+        p_copy(b, 1, hp_c).wait_send()
+        px_copy(b).wait_send()
+        a_copy(b, 0, hp).wait_send()
+        a_copy(b, 1, hp).wait_send()
+        a_copy(b, 2, hp_x).wait_send()
         for e in range(nz):
             @pl.when(jnp.logical_and(z >= e, right_ok))
             def _():
@@ -538,7 +558,8 @@
             pltpu.VMEM((nz, rows, cols), bf16),
             pltpu.VMEM((nz, rows, cols), bf16),
             pltpu.VMEM((nz, rows, cols), bf16),
-            pltpu.VMEM((nz, nhp, part_rows, cols), bf16),
+            pltpu.VMEM((nz, part_rows, cols), bf16),
+            pltpu.VMEM((nz, 3, part_rows, cols), bf16),
             pltpu.VMEM((nhp, part_rows, cols), bf16),
             pltpu.VMEM((nz, part_rows, cols), bf16),
             pltpu.VMEM((nz, nz, rows, cols), bf16),
@@ -551,12 +572,12 @@
             dma((nhp,)), dma((nhp,)),
             dma((nz,)), dma((nz,)),
             dma((nz, 2, 2)), dma((nz, 2)),
-            dma((nz, nhp)), dma((nz, nhp)),
+            dma((nz, 3)), dma((nz, 3)),
             dma((nz, nz, 2)), dma((nz, nz)),
             dma((nz, nz)), dma((nz, nz)),
             dma((nz, nz)), dma((nz, nz)),
             dma((nz, nz)), dma((nz, nz)),
-            dma((nz, nhp)), dma((nz, nhp)),
+            dma((nz, 3)), dma((nz, 3)),
             dma((nz,)), dma((nz,)),
         ],
         compiler_params=pltpu.CompilerParams(

time: 105 us -> 102 us (0.971)
  Pallas kernels: 101 us -> 97.2 us
    pallas_call x1, Pallas kernels: 101 us -> 97.2 us  [fused_body(): pl.pallas_call(functools.partial(fused_kernel, nz, nx, npair), out_shape=...]
where the time goes in v4:
time: 102 us; the launch traced here: 101 us
  Pallas kernels  97.2 us (95%)
  local copies, waits for them, and re-layouts  3.34 us (3%)
    pallas_call x1, Pallas kernels, fused_body(): pl.pallas_call(functools.partial(fused_kernel, nz, nx, npair), out_shape=...  97.2 us
    unnamed x2, local copies, waits for them, and re-layouts  3.34 us

profile of v4, /device:TPU:25, one launch (start us, length us, event | category | flops | bytes accessed | tf_op | source)
XLA Modules:
  0.0 101.2 jit_solution(13283748246541342068)
XLA Ops:
  0.6 97.2 %shard_map.113 = (bf16[128,1024]{1,0:T(8,128)(2,1)}, bf16[128,1024]{1,0:T(8,128)(2,1)}) custom-call(bf16[128,1024]{1,0:T(8,128)(2,1)} %q_hbm.1, bf16[2,128,256]{2,1,0:T(8,128)(2,1)} %kv_hbm.1, bf16[128,1024]{1,0:T(8,128)(2,1)} %resid_hbm.1, f32[4,1,1024]{2,1,0:T(1,128)} %bitcast.3, s32[2,128]{1,0:T(2,128)} %bitcast.4, f32[2,128]{1,0:T(2,128)} %bitcast.5, ...), custom_call_target="tpu_custom_call" | custom-call | flops 4294967296 | bytes 8388608 | tf_op jit(solution)/shard_map/pallas_call | solution.py:545
  97.9 1.7 %copy.14 = bf16[128,1024]{1,0:T(8,128)(2,1)} copy(bf16[128,1024]{1,0:T(8,128)(2,1)} %get-tuple-element.4) | data formatting | bytes 524288
  99.5 1.7 %copy.15 = bf16[128,1024]{1,0:T(8,128)(2,1)} copy(bf16[128,1024]{1,0:T(8,128)(2,1)} %get-tuple-element.5) | data formatting | bytes 524288

commit v5 on v4

--- a/solution.py
+++ b/solution.py
@@ -232,8 +232,6 @@
     own_resid.wait()
     for other in hp_others:
         resid_wait(other).wait_recv()
-    for i in range(nz - 1):
-        resid_along(i).start()
     resid_t[z] = resid_s[z]
 
     for copy in small:
@@ -270,8 +268,8 @@
     def px_copy(b):
         return remote(psum.at[b], pin.at[b, 2], p_s.at[b, 2], p_r.at[b, 2], x_dev)
 
-    def z_copy(b, e, way, dev):
-        return same(xall.at[b, e, mine], z_s.at[b, e, way], z_r.at[b, e], at(dev, hp))
+    def z_copy(b, i):
+        return same(xall.at[b, z, mine], z_s.at[b, i], z_r.at[b, z], at(z_others[i], hp))
 
     def x_copy(b, e, owner):
         return same(xall.at[b, e, slab(owner)], x_s.at[b, e], x_r.at[b, e], x_dev)
@@ -326,43 +324,16 @@
         total = pbuf[b, mine, :].astype(f32) + pin[b, 1].astype(f32) + pin[b, 2].astype(f32)
         xall[b, z, mine, :] = (resid_t[b].astype(f32) + total).astype(bf16)
 
-        @pl.when(right_ok)
-        def _():
-            z_copy(b, z, 0, right).start()
-
-        @pl.when(left_ok)
-        def _():
-            z_copy(b, z, 1, left).start()
-
+        for i in range(nz - 1):
+            z_copy(b, i).start()
         x_copy(b, z, hp).start()
         c_copy(b, z, hp).start()
 
-    def spread(b, d):
-        @pl.when(z >= d)
-        def _():
-            z_copy(b, z - d, 0, right).wait_recv()
-
-        @pl.when(jnp.logical_and(z >= d, right_ok))
-        def _():
-            z_copy(b, z - d, 0, right).start()
-
-        @pl.when(z + d < nz)
-        def _():
-            z_copy(b, z + d, 1, left).wait_recv()
-
-        @pl.when(jnp.logical_and(z + d < nz, left_ok))
-        def _():
-            z_copy(b, z + d, 1, left).start()
-
-        @pl.when(z >= d)
-        def _():
-            x_copy(b, z - d, hp).start()
-            c_copy(b, z - d, hp).start()
-
-        @pl.when(z + d < nz)
-        def _():
-            x_copy(b, z + d, hp).start()
-            c_copy(b, z + d, hp).start()
+    def spread(b):
+        for other in z_others:
+            same(xall.at[b, other, mine], z_s.at[b, 0], z_r.at[b, other], at(other, hp)).wait_recv()
+            x_copy(b, other, hp).start()
+            c_copy(b, other, hp).start()
 
     def pass_on(b):
         for e in range(nz):
@@ -423,6 +394,8 @@
 
     for d in range(2, nz - 1):
         query_hop(d)
+    for i in range(nz - 1):
+        resid_along(i).start()
 
     @pl.when(near_first)
     def _():
@@ -436,42 +409,40 @@
         project(b)
     for b in first:
         pair_sum(b)
+    for b in first:
+        add_up(b)
     query_hop(nz - 1)
     attend(last[0])
     project(last[0])
     for b in first:
-        add_up(b)
+        spread(b)
     pair_sum(last[0])
     attend(last[1])
     project(last[1])
+    add_up(last[0])
     for b in first:
-        spread(b, 1)
-    add_up(last[0])
+        pass_on(b)
     pair_sum(last[1])
-    for b in first:
-        spread(b, 2)
     add_up(last[1])
-    spread(last[0], 1)
-    for b in first:
-        spread(b, 3)
-    spread(last[1], 1)
-    spread(last[0], 2)
-    pass_on(first[0])
-    spread(last[1], 2)
-    for b in last:
-        spread(b, 3)
     weights[1].wait()
     weights[2].wait()
     weights[3].wait()
-    for i in range(nz + 1):
-        if i + 1 < nz:
-            pass_on(order[i + 1])
-        if i < nz:
-            hidden_units(order[i])
-        if i >= 1:
-            down(order[i - 1])
-        if i < nz:
-            act_pass(order[i])
+    hidden_units(first[0])
+    spread(last[0])
+    act_pass(first[0])
+    hidden_units(first[1])
+    spread(last[1])
+    pass_on(last[0])
+    down(first[0])
+    act_pass(first[1])
+    pass_on(last[1])
+    hidden_units(last[0])
+    down(first[1])
+    act_pass(last[0])
+    hidden_units(last[1])
+    down(last[0])
+    act_pass(last[1])
+    down(last[1])
 
     hid_ref[...] = xall[z, hp]
     diagonal = lax.broadcasted_iota(jnp.int32, (rows, rows), 0) == lax.broadcasted_iota(
@@ -509,15 +480,9 @@
         a_copy(b, 0, hp).wait_send()
         a_copy(b, 1, hp).wait_send()
         a_copy(b, 2, hp_x).wait_send()
+        for i in range(nz - 1):
+            z_copy(b, i).wait_send()
         for e in range(nz):
-            @pl.when(jnp.logical_and(z >= e, right_ok))
-            def _():
-                z_copy(b, e, 0, right).wait_send()
-
-            @pl.when(jnp.logical_and(z <= e, left_ok))
-            def _():
-                z_copy(b, e, 1, left).wait_send()
-
             x_copy(b, e, hp).wait_send()
             c_copy(b, e, hp).wait_send()
             f_copy(b, e, hp_x).wait_send()
@@ -573,7 +538,7 @@
             dma((nz,)), dma((nz,)),
             dma((nz, 2, 2)), dma((nz, 2)),
             dma((nz, 3)), dma((nz, 3)),
-            dma((nz, nz, 2)), dma((nz, nz)),
+            dma((nz, nz)), dma((nz, nz)),
             dma((nz, nz)), dma((nz, nz)),
             dma((nz, nz)), dma((nz, nz)),
             dma((nz, nz)), dma((nz, nz)),

time: 102 us -> 100 us (0.980)
  Pallas kernels: 97.2 us -> 94.4 us
    pallas_call x1, Pallas kernels: 97.2 us -> 94.4 us  [fused_body(): pl.pallas_call(functools.partial(fused_kernel, nz, nx, npair), out_shape=...]
where the time goes in v5:
time: 100 us; the launch traced here: 98.4 us
  Pallas kernels  94.4 us (94%)
  local copies, waits for them, and re-layouts  3.34 us (3%)
    pallas_call x1, Pallas kernels, fused_body(): pl.pallas_call(functools.partial(fused_kernel, nz, nx, npair), out_shape=...  94.4 us
    unnamed x2, local copies, waits for them, and re-layouts  3.34 us

profile of v5, /device:TPU:25, one launch (start us, length us, event | category | flops | bytes accessed | tf_op | source)
XLA Modules:
  0.0 98.4 jit_solution(8141658366712171918)
XLA Ops:
  0.6 94.4 %shard_map.113 = (bf16[128,1024]{1,0:T(8,128)(2,1)}, bf16[128,1024]{1,0:T(8,128)(2,1)}) custom-call(bf16[128,1024]{1,0:T(8,128)(2,1)} %q_hbm.1, bf16[2,128,256]{2,1,0:T(8,128)(2,1)} %kv_hbm.1, bf16[128,1024]{1,0:T(8,128)(2,1)} %resid_hbm.1, f32[4,1,1024]{2,1,0:T(1,128)} %bitcast.3, s32[2,128]{1,0:T(2,128)} %bitcast.4, f32[2,128]{1,0:T(2,128)} %bitcast.5, ...), custom_call_target="tpu_custom_call" | custom-call | flops 4294967296 | bytes 8388608 | tf_op jit(solution)/shard_map/pallas_call | solution.py:510
  95.1 1.7 %copy.14 = bf16[128,1024]{1,0:T(8,128)(2,1)} copy(bf16[128,1024]{1,0:T(8,128)(2,1)} %get-tuple-element.4) | data formatting | bytes 524288
  96.8 1.7 %copy.15 = bf16[128,1024]{1,0:T(8,128)(2,1)} copy(bf16[128,1024]{1,0:T(8,128)(2,1)} %get-tuple-element.5) | data formatting | bytes 524288

commit v6 on v5

--- a/solution.py
+++ b/solution.py
@@ -286,10 +286,14 @@
     def e_copy(b):
         return remote(eo.at[b], ret.at[z], e_s.at[b], e_r.at[z], at(b, hp))
 
-    def project(b):
-        pbuf[b] = jnp.dot(ho[b], wo[...], preferred_element_type=f32).astype(bf16)
-        p_copy(b, 0, hp_xc).start()
-        p_copy(b, 1, hp_c).start()
+    def project(*blocks):
+        shares = jnp.dot(
+            jnp.concatenate([ho[b] for b in blocks], axis=0), wo[...], preferred_element_type=f32
+        ).astype(bf16)
+        for i, b in enumerate(blocks):
+            pbuf[b] = shares[i * rows : (i + 1) * rows]
+            p_copy(b, 0, hp_xc).start()
+            p_copy(b, 1, hp_c).start()
 
     def pair_sum(b):
         p_copy(b, 0, hp_xc).wait_recv()
@@ -340,41 +344,51 @@
             x_copy(b, e, hp_x).wait_recv()
             f_copy(b, e, hp_x).start()
 
-    def hidden_units(b):
+    def hidden_units(*blocks):
+        roots = []
+        for b in blocks:
+            square = jnp.zeros((rows, 1), f32)
+            for e in range(nz):
+                c_copy(b, e, hp_c).wait_recv()
+                f_copy(b, e, hp_xc).wait_recv()
+                part = xall[b, e].astype(f32)
+                square = square + jnp.sum(part * part, axis=1, keepdims=True)
+            roots.append(lax.rsqrt(square / D + norm_eps))
+        both = jnp.zeros((len(blocks) * rows, 2 * hidden), f32)
         for e in range(nz):
-            c_copy(b, e, hp_c).wait_recv()
-            f_copy(b, e, hp_xc).wait_recv()
-        square = jnp.zeros((rows, 1), f32)
-        for e in range(nz):
-            part = xall[b, e].astype(f32)
-            square = square + jnp.sum(part * part, axis=1, keepdims=True)
-        root = lax.rsqrt(square / D + norm_eps)
-        both = jnp.zeros((rows, 2 * hidden), f32)
-        for e in range(nz):
-            normed = (xall[b, e].astype(f32) * root * gain_ref[e]).astype(bf16)
+            normed = jnp.concatenate(
+                [
+                    (xall[b, e].astype(f32) * root * gain_ref[e]).astype(bf16)
+                    for b, root in zip(blocks, roots)
+                ],
+                axis=0,
+            )
             both = both + jnp.dot(normed, wgu[e * cols : (e + 1) * cols, :], preferred_element_type=f32)
         gate, up = both[:, :hidden], both[:, hidden:]
-        act_all[b, hp] = (gate / (1.0 + jnp.exp(-gate)) * up).astype(bf16)
-        a_copy(b, 0, hp).start()
-        a_copy(b, 1, hp).start()
+        activated = (gate / (1.0 + jnp.exp(-gate)) * up).astype(bf16)
+        for i, b in enumerate(blocks):
+            act_all[b, hp] = activated[i * rows : (i + 1) * rows]
+            a_copy(b, 0, hp).start()
+            a_copy(b, 1, hp).start()
 
     def act_pass(b):
         a_copy(b, 0, hp_x).wait_recv()
         a_copy(b, 2, hp_x).start()
 
-    def down(b):
-        a_copy(b, 1, hp_c).wait_recv()
-        a_copy(b, 2, hp_xc).wait_recv()
-        total = jnp.zeros((rows, cols), f32)
+    def down(*blocks):
+        for b in blocks:
+            a_copy(b, 1, hp_c).wait_recv()
+            a_copy(b, 2, hp_xc).wait_recv()
+        total = jnp.zeros((len(blocks) * rows, cols), f32)
         for j in range(nhp):
-            total = total + jnp.dot(
-                act_all[b, j], wd[j * hidden : (j + 1) * hidden, :], preferred_element_type=f32
-            )
-        eo[b] = total.astype(bf16)
-
-        @pl.when(z != b)
-        def _():
-            e_copy(b).start()
+            units = jnp.concatenate([act_all[b, j] for b in blocks], axis=0)
+            total = total + jnp.dot(units, wd[j * hidden : (j + 1) * hidden, :], preferred_element_type=f32)
+        for i, b in enumerate(blocks):
+            eo[b] = total[i * rows : (i + 1) * rows].astype(bf16)
+
+            @pl.when(z != b)
+            def _():
+                e_copy(b).start()
 
     order = sorted(range(nz), key=lambda b: max(b, nz - 1 - b))
     first, last = order[: nz // 2], order[nz // 2 :]
@@ -405,8 +419,7 @@
     def _():
         attend(first[0])
 
-    for b in first:
-        project(b)
+    project(*first)
     for b in first:
         pair_sum(b)
     for b in first:
@@ -427,22 +440,18 @@
     weights[1].wait()
     weights[2].wait()
     weights[3].wait()
-    hidden_units(first[0])
-    spread(last[0])
-    act_pass(first[0])
-    hidden_units(first[1])
-    spread(last[1])
-    pass_on(last[0])
-    down(first[0])
-    act_pass(first[1])
-    pass_on(last[1])
-    hidden_units(last[0])
-    down(first[1])
-    act_pass(last[0])
-    hidden_units(last[1])
-    down(last[0])
-    act_pass(last[1])
-    down(last[1])
+    hidden_units(*first)
+    for b in last:
+        spread(b)
+    for b in first:
+        act_pass(b)
+    down(*first)
+    for b in last:
+        pass_on(b)
+    hidden_units(*last)
+    for b in last:
+        act_pass(b)
+    down(*last)
 
     hid_ref[...] = xall[z, hp]
     diagonal = lax.broadcasted_iota(jnp.int32, (rows, rows), 0) == lax.broadcasted_iota(

time: 100 us -> 103 us (1.030)
  the two profiles are of different devices: /device:TPU:25 before, /device:TPU:0 now
where the time goes in v6:
time: 103 us
  Pallas kernels  99.2 us (96%)
  local copies, waits for them, and re-layouts  3.34 us (3%)
    pallas_call x1, Pallas kernels, fused_body(): pl.pallas_call(functools.partial(fused_kernel, nz, nx, npair), out_shape=...  99.2 us
    unnamed x2, local copies, waits for them, and re-layouts  3.34 us

profile of v6, /device:TPU:0, one launch (start us, length us, event | category | flops | bytes accessed | tf_op | source)
XLA Modules:
  0.0 103.2 jit_solution(7197613198484188043)
XLA Ops:
  0.6 99.2 %shard_map.113 = (bf16[128,1024]{1,0:T(8,128)(2,1)}, bf16[128,1024]{1,0:T(8,128)(2,1)}) custom-call(bf16[128,1024]{1,0:T(8,128)(2,1)} %q_hbm.1, bf16[2,128,256]{2,1,0:T(8,128)(2,1)} %kv_hbm.1, bf16[128,1024]{1,0:T(8,128)(2,1)} %resid_hbm.1, f32[4,1,1024]{2,1,0:T(1,128)} %bitcast.3, s32[2,128]{1,0:T(2,128)} %bitcast.4, f32[2,128]{1,0:T(2,128)} %bitcast.5, ...), custom_call_target="tpu_custom_call" | custom-call | flops 4294967296 | bytes 8388608 | tf_op jit(solution)/shard_map/pallas_call | solution.py:519
  99.8 1.7 %copy.14 = bf16[128,1024]{1,0:T(8,128)(2,1)} copy(bf16[128,1024]{1,0:T(8,128)(2,1)} %get-tuple-element.4) | data formatting | bytes 524288
  101.5 1.7 %copy.15 = bf16[128,1024]{1,0:T(8,128)(2,1)} copy(bf16[128,1024]{1,0:T(8,128)(2,1)} %get-tuple-element.5) | data formatting | bytes 524288

commit v7 on v5

--- a/solution.py
+++ b/solution.py
@@ -428,21 +428,21 @@
     weights[2].wait()
     weights[3].wait()
     hidden_units(first[0])
-    spread(last[0])
+    for b in last:
+        spread(b)
     act_pass(first[0])
-    hidden_units(first[1])
-    spread(last[1])
     pass_on(last[0])
     down(first[0])
-    act_pass(first[1])
     pass_on(last[1])
     hidden_units(last[0])
-    down(first[1])
     act_pass(last[0])
     hidden_units(last[1])
     down(last[0])
     act_pass(last[1])
+    hidden_units(first[1])
     down(last[1])
+    act_pass(first[1])
+    down(first[1])
 
     hid_ref[...] = xall[z, hp]
     diagonal = lax.broadcasted_iota(jnp.int32, (rows, rows), 0) == lax.broadcasted_iota(

time: 100 us -> 106 us (1.060)
  the two profiles are of different devices: /device:TPU:25 before, /device:TPU:19 now
where the time goes in v7:
time: 106 us
  Pallas kernels  102 us (96%)
  local copies, waits for them, and re-layouts  3.34 us (3%)
    pallas_call x1, Pallas kernels, fused_body(): pl.pallas_call(functools.partial(fused_kernel, nz, nx, npair), out_shape=...  102 us
    unnamed x2, local copies, waits for them, and re-layouts  3.34 us

profile of v7, /device:TPU:19, one launch (start us, length us, event | category | flops | bytes accessed | tf_op | source)
XLA Modules:
  0.0 105.8 jit_solution(4226040263067968709)
XLA Ops:
  0.6 101.9 %shard_map.113 = (bf16[128,1024]{1,0:T(8,128)(2,1)}, bf16[128,1024]{1,0:T(8,128)(2,1)}) custom-call(bf16[128,1024]{1,0:T(8,128)(2,1)} %q_hbm.1, bf16[2,128,256]{2,1,0:T(8,128)(2,1)} %kv_hbm.1, bf16[128,1024]{1,0:T(8,128)(2,1)} %resid_hbm.1, f32[4,1,1024]{2,1,0:T(1,128)} %bitcast.3, s32[2,128]{1,0:T(2,128)} %bitcast.4, f32[2,128]{1,0:T(2,128)} %bitcast.5, ...), custom_call_target="tpu_custom_call" | custom-call | flops 4294967296 | bytes 8388608 | tf_op jit(solution)/shard_map/pallas_call | solution.py:510
  102.5 1.7 %copy.14 = bf16[128,1024]{1,0:T(8,128)(2,1)} copy(bf16[128,1024]{1,0:T(8,128)(2,1)} %get-tuple-element.4) | data formatting | bytes 524288
  104.2 1.7 %copy.15 = bf16[128,1024]{1,0:T(8,128)(2,1)} copy(bf16[128,1024]{1,0:T(8,128)(2,1)} %get-tuple-element.5) | data formatting | bytes 524288
